TPU v7x, 32 devices: a whole 2x2x4 slice. The times are simulated.
32 devices in a mesh: lo: 8 (over z, y), hi: 4 (over x, core).
Axes of the slice: x: 2, y: 2, z: 4, core: 2. Of those that a mesh axis runs over, the one named last changes fastest.
Arguments:
- contribution: float32 [4, 8, 1024, 1024], P('hi', 'lo'), as said below
- pivot_one: float32 [4, 8, 384, 768], P('hi', 'lo'), as said below
- rows_one: float32 [4, 8, 768, 2304], P('hi', 'lo'), as said below
- pivot_two: float32 [4, 8, 192, 768], P('hi', 'lo'), as said below
- rows_two: float32 [4, 8, 384, 2304], P('hi', 'lo'), as said below
- map_one: int32 [4, 8, 8], replicated, may hold values from 0 to 17, as said below
- map_two: int32 [4, 4, 12], replicated, may hold values from 0 to 17, as said below
- fill_one: int32 [4, 4, 12, 6], replicated, may hold values 0 or 1
- fill_two: int32 [2, 4, 12, 6], replicated, may hold values 0 or 1
- live_one: int32 [4, 4], replicated, may hold values from 3 to 6, as said below
- live_two: int32 [2, 4], replicated, may hold values from 3 to 6, as said below
Outputs:
- lower_one: float32 [4, 8, 384, 768], P('hi', 'lo')
- panel_one: float32 [4, 8, 768, 768], P('hi', 'lo')
- lower_two: float32 [4, 8, 192, 768], P('hi', 'lo')
- panel_two: float32 [4, 8, 384, 768], P('hi', 'lo')
- schur_two: float32 [4, 8, 384, 1536], P('hi', 'lo')
Inputs may be any that keep to these rules, and one draw needn't show every extreme that they name: `contribution`: symmetric and negative semidefinite: minus a Gram matrix, divided by 1024. `pivot_one`: with rows_one, the rows of a symmetric matrix of each front with a dominant diagonal. `rows_one`: with pivot_one, the rows of a symmetric matrix of each front with a dominant diagonal. `pivot_two`: with rows_two, the rows of a symmetric matrix of each front with a dominant diagonal. `rows_two`: with pivot_two, the rows of a symmetric matrix of each front with a dominant diagonal. `map_one`: each device's list names 8 distinct tiles. `map_two`: each front's list names 12 distinct tiles. `live_one`: both ends reached in every draw. `live_two`: both ends reached in every draw.
All inputs are finite; a program needn't handle non-finite values.
Results may differ from a plain program's by a relative error of at most 0.0003.
Values sent between devices are 32-bit elements; how exact they have to be, the bound alone decides.
No kernel may reach another device: no remote copies, remote signals or barrier semaphores. Data moves between devices by JAX's collectives and lax.ppermute only.
A program may use at most 192 MiB of HBM per device.

v0:
```python
import jax
import jax.numpy as jnp
from jax import lax
from jax.sharding import PartitionSpec as P

TILE = 128
P1T = 6
U1T = 12
P2T = 6
U2T = 12


HIGHEST_MODE = lax.Precision.HIGHEST


def partner(array, axis, apart):
    return lax.ppermute(array, axis, [(i, i ^ 1 << apart) for i in range(lax.axis_size(axis))])


def spread(source_block, row_map, col_map, row_first, row_tiles, col_tiles):
    row_count = row_map.shape[0]
    col_count = col_map.shape[0]
    tile_size = source_block.shape[1] // col_count
    targets = row_first + jnp.arange(row_tiles, dtype=jnp.int32)
    row_onehot = (row_map[:, None] == targets[None, :]).astype(jnp.float32)
    col_onehot = (col_map[:, None] == jnp.arange(col_tiles, dtype=jnp.int32)[None, :]).astype(
        jnp.float32
    )
    blocks = source_block.reshape(row_count, tile_size, col_count, tile_size)
    placed = jnp.einsum("ia,ixky->axky", row_onehot, blocks, precision=HIGHEST_MODE)
    placed = jnp.einsum("axky,kb->axby", placed, col_onehot, precision=HIGHEST_MODE)
    return placed.reshape(row_tiles * tile_size, col_tiles * tile_size)


def factor(pivot_block, coupling, live_tiles):
    kept = (jnp.arange(pivot_block.shape[0]) // TILE < live_tiles).astype(pivot_block.dtype)
    pivot_block = pivot_block * kept[:, None] * kept[None, :] + jnp.diag(1.0 - kept)
    coupling = coupling * kept[None, :]
    factor_lower = jnp.linalg.cholesky(pivot_block)
    panel_part = lax.linalg.triangular_solve(
        factor_lower, coupling, left_side=False, lower=True, transpose_a=True
    )
    return (factor_lower, panel_part)


def expand_fill(fill_tiles):
    return jnp.repeat(jnp.repeat(fill_tiles, TILE, axis=0), TILE, axis=1).astype(jnp.float32)


def across_lo(values_in):
    return partner(values_in, "lo", lax.axis_size("lo").bit_length() - 2)


def across_hi(values_in):
    return partner(values_in, "hi", lax.axis_size("hi").bit_length() - 2)


def ordered(mine, theirs, which_side):
    first_half = jnp.where(which_side == 0, mine, theirs)
    second_half = jnp.where(which_side == 0, theirs, mine)
    return jnp.concatenate([first_half, second_half], axis=0)


def body(
    contribution,
    pivot_one,
    rows_one,
    pivot_two,
    rows_two,
    map_one,
    map_two,
    fill_one,
    fill_two,
    live_one,
    live_two,
):
    size_lo = lax.axis_size("lo")
    size_hi = lax.axis_size("hi")
    half_lo = size_lo // 2
    half_hi = size_hi // 2
    index_lo = lax.axis_index("lo")
    index_hi = lax.axis_index("hi")
    side_lo = index_lo // half_lo
    side_hi = index_hi // half_hi
    front_lo = index_lo % half_lo
    front_hi = index_hi % half_hi
    pivot_size = P1T * TILE
    half_tiles = U1T // 2
    own_block = contribution[0, 0]
    own_map = map_one[index_hi, index_lo]
    own_pivot = pivot_one[0, 0]
    fill_tiles = lax.dynamic_slice_in_dim(
        fill_one[index_hi, front_lo], side_lo * half_tiles, half_tiles, 0
    )
    own_rows = rows_one[0, 0]
    own_rows = jnp.concatenate(
        [own_rows[:, :pivot_size] * expand_fill(fill_tiles), own_rows[:, pivot_size:]], axis=1
    )
    own_start = P1T + side_lo * half_tiles
    placed_pivot = lax.dynamic_update_slice(
        jnp.zeros((pivot_size, pivot_size), jnp.float32),
        own_pivot,
        (side_lo * (pivot_size // 2), 0),
    )
    other_block, other_pivot = partner((own_block, own_pivot), "lo", size_lo.bit_length() - 2)
    other_map = map_one[index_hi, (index_lo + half_lo) % size_lo]
    placed_pivot = lax.dynamic_update_slice(
        placed_pivot, other_pivot, ((1 - side_lo) * (pivot_size // 2), 0)
    )
    pivot_block = (
        placed_pivot
        + spread(own_block, own_map, own_map, 0, P1T, P1T)
        + spread(other_block, other_map, other_map, 0, P1T, P1T)
    )
    front_rows = (
        own_rows
        + spread(own_block, own_map, own_map, own_start, half_tiles, P1T + U1T)
        + spread(other_block, other_map, other_map, own_start, half_tiles, P1T + U1T)
    )
    factor_lower, panel_part = factor(
        pivot_block, front_rows[:, :pivot_size], live_one[index_hi, front_lo]
    )
    full_panel = ordered(panel_part, across_lo(panel_part), side_lo)
    schur_rows = front_rows[:, pivot_size:] - jnp.dot(
        panel_part, full_panel.T, precision=HIGHEST_MODE
    )
    lower_one = lax.dynamic_slice_in_dim(
        factor_lower, side_lo * (pivot_size // 2), pivot_size // 2, 0
    )
    second_size = P2T * TILE
    quarter_tiles = U2T // 4
    quarter_rows = quarter_tiles * TILE
    quarter_pivot = second_size // 4
    second_width = (P2T + U2T) * TILE
    quarter = 2 * side_hi + side_lo
    second_map = map_two[index_hi, front_lo]
    row_map = lax.dynamic_slice_in_dim(second_map, side_lo * half_tiles, half_tiles, 0)
    pivot_part = lax.dynamic_update_slice(
        jnp.zeros((second_size, second_size), jnp.float32),
        pivot_two[0, 0],
        (quarter * quarter_pivot, 0),
    )
    pivot_part = pivot_part + spread(schur_rows, row_map, second_map, 0, P2T, P2T)
    part_rows = spread(schur_rows, row_map, second_map, P2T, U2T, P2T + U2T)
    grouped = part_rows.reshape(2, 2 * quarter_rows, second_width)
    got_pivot, got_rows = across_hi((pivot_part, grouped[1 - side_hi]))
    pivot_part = pivot_part + got_pivot
    kept_rows = (grouped[side_hi] + got_rows).reshape(2, quarter_rows, second_width)
    got_pivot, got_rows = across_lo((pivot_part, kept_rows[1 - side_lo]))
    second_pivot = pivot_part + got_pivot
    quarter_part = kept_rows[side_lo] + got_rows
    fill_second = lax.dynamic_slice_in_dim(
        fill_two[front_hi, front_lo], quarter * quarter_tiles, quarter_tiles, 0
    )
    own_second = rows_two[0, 0]
    quarter_part = quarter_part + jnp.concatenate(
        [own_second[:, :second_size] * expand_fill(fill_second), own_second[:, second_size:]],
        axis=1,
    )
    lower_full, panel_two = factor(
        second_pivot, quarter_part[:, :second_size], live_two[front_hi, front_lo]
    )
    pair_panel = ordered(panel_two, across_lo(panel_two), side_lo)
    all_panel = ordered(pair_panel, across_hi(pair_panel), side_hi)
    schur_two = quarter_part[:, second_size:] - jnp.dot(
        panel_two, all_panel.T, precision=HIGHEST_MODE
    )
    lower_two = lax.dynamic_slice_in_dim(lower_full, quarter * quarter_pivot, quarter_pivot, 0)
    return (
        lower_one[None, None],
        panel_part[None, None],
        lower_two[None, None],
        panel_two[None, None],
        schur_two[None, None],
    )


def solution(mesh):
    placed = (
        P("hi", "lo", None, None),
        P("hi", "lo", None, None),
        P("hi", "lo", None, None),
        P("hi", "lo", None, None),
        P("hi", "lo", None, None),
        P(),
        P(),
        P(),
        P(),
        P(),
        P(),
    )
    return jax.shard_map(
        body,
        mesh=mesh,
        in_specs=placed,
        out_specs=(
            P("hi", "lo", None, None),
            P("hi", "lo", None, None),
            P("hi", "lo", None, None),
            P("hi", "lo", None, None),
            P("hi", "lo", None, None),
        ),
        check_vma=False,
    )
```

profile of v0, /device:TPU:0, one launch (start us, length us, event | category | flops | bytes accessed | tf_op | source)
XLA Modules:
  0.0 1304.5 jit_solution(14358586176486666793)
XLA Ops:
  13.4 6.5 fusion.20
  28.7 8.2 copy.188
  36.9 8.0 copy.183
  50.0 6.8 fusion.22
  69.9 166.1 %collective-permute-done = f32[384,768]{0,1:T(8,128)} collective-permute-done((f32[384,768]{0,1:T(8,128)}, f32[384,768]{0,1:T(8,128)}, u32[]{:S(2)}, u32[]{:S(2)}) %collective-permute-start) | collective-permute-done | bytes 1179680 | tf_op jit(solution)/shard_map/ppermute | solution.py:17
  261.6 8.0 copy.191
  278.8 7.2 fusion.5
  296.4 11.7 cholesky.453
  308.3 9.8 custom-call.45
  321.1 11.7 cholesky.472
  332.9 10.0 custom-call.46
  345.5 11.7 cholesky.493
  357.4 9.8 custom-call.47
  369.7 12.1 cholesky.512
  381.9 9.8 custom-call.48
  394.0 11.7 cholesky.531
  405.9 9.8 custom-call.49
  417.7 11.7 cholesky.548
  439.2 18.1 %while.2 = (s32[]{:T(128)}, f32[768,768]{0,1:T(8,128)}, s32[6,2]{0,1:T(2,128)S(1)}, f32[6,128,128]{2,1,0:T(8,128)S(1)}, s32[]{:T(128)}) while((s32[]{:T(128)}, f32[768,768]{0,1:T(8,128)}, s32[6,2]{0,1:T(2,128)S(1)}, f32[6,128,128]{2,1,0:T(8,128)S(1)}, s32[]{:T(128)}) %tuple.86), condition=%wide.while_cond, body=%wide.while_body.sunk | while | flops 2 | bytes 393329 | solution.py:40
  457.3 59.2 %custom-call.38 = f32[6,128,128]{1,2,0:T(8,128)S(1)} custom-call(f32[6,128,128]{2,1,0:T(8,128)S(1)} %get-tuple-element.13), custom_call_target="InvertDiagBlocksLowerTriangular" | custom-call | tf_op jit(solution)/shard_map/triangular_solve | solution.py:40
  539.2 101.6 %collective-permute-done.2 = f32[768,768]{0,1:T(8,128)} collective-permute-done((f32[768,768]{0,1:T(8,128)}, f32[768,768]{0,1:T(8,128)}, u32[]{:S(2)}, u32[]{:S(2)}) %collective-permute-start.2) | collective-permute-done | bytes 2359328 | tf_op jit(solution)/shard_map/ppermute | solution.py:17
  643.5 25.4 %slice_subtract_fusion = f32[768,1536]{0,1:T(8,128)} fusion(f32[768,2304]{0,1:T(8,128)S(1)} %bitcast.305, f32[768,768]{0,1:T(8,128)} %convolution_dynamic-update-slice_fusion, f32[768,768]{0,1:T(8,128)S(1)} %get-tuple-element.101, f32[768,768]{0,1:T(8,128)S(1)} %get-tuple-element.100), kind=kOutput, calls=%fused_computation.15 | convolution fusion | flops 10873995264 | bytes 16515072 | tf_op jit(solution)/shard_map/dot_general | solution.py:124
  668.9 6.6 reshape.226
  675.5 6.7 copy.200
  695.5 6.6 add.233
  702.8 7.9 fusion.185
  710.7 14.6 %fusion.2 = f32[12,128,18,128]{3,2,1,0:T(8,128)} fusion(f32[12,128,12,128]{3,0,2,1:T(8,128)S(1)} %fusion.185, s32[12]{0:T(128)S(1)} %fusion.208), kind=kOutput, calls=%fused_computation.6 | convolution fusion | flops 509608160 | bytes 23593008 | tf_op jit(solution)/shard_map/axky,kb->axby/dot_general | solution.py:31
  725.3 17.8 %reshape_reshape.3 = f32[2,768,2304]{2,1,0:T(8,128)} reshape(f32[12,128,18,128]{3,2,1,0:T(8,128)} %fusion.2) | data formatting | bytes 28311552 | tf_op jit(solution)/shard_map/reshape;reshape | solution.py:145
  743.1 10.7 collective-permute-done.3
  757.5 6.4 dynamic-slice_bitcast_fusion
  773.3 86.2 %collective-permute-done.4 = f32[768,768]{0,1:T(8,128)} collective-permute-done((f32[768,768]{0,1:T(8,128)}, f32[768,768]{0,1:T(8,128)}, u32[]{:S(2)}, u32[]{:S(2)}) %collective-permute-start.4) | collective-permute-done | bytes 2359328 | tf_op jit(solution)/shard_map/ppermute | solution.py:17
  868.0 11.7 cholesky.563
  879.8 9.8 custom-call.50
  892.6 11.7 cholesky.582
  904.5 10.0 custom-call.51
  917.0 11.7 cholesky.603
  928.9 9.8 custom-call.52
  941.2 11.9 cholesky.622
  953.2 9.8 custom-call.53
  965.3 11.7 cholesky.641
  977.2 9.8 custom-call.54
  989.2 11.7 cholesky.658
  1021.2 18.1 %while.3 = (s32[]{:T(128)}, f32[768,768]{0,1:T(8,128)}, s32[6,2]{0,1:T(2,128)S(1)}, f32[6,128,128]{2,1,0:T(8,128)S(1)}, s32[]{:T(128)}) while((s32[]{:T(128)}, f32[768,768]{0,1:T(8,128)}, s32[6,2]{0,1:T(2,128)S(1)}, f32[6,128,128]{2,1,0:T(8,128)S(1)}, s32[]{:T(128)}) %tuple.92), condition=%wide.while_cond.1, body=%wide.while_body.1.sunk | while | flops 2 | bytes 393329 | solution.py:40
  1039.3 59.1 %custom-call.39 = f32[6,128,128]{1,2,0:T(8,128)S(1)} custom-call(f32[6,128,128]{2,1,0:T(8,128)S(1)} %get-tuple-element.21), custom_call_target="InvertDiagBlocksLowerTriangular" | custom-call | tf_op jit(solution)/shard_map/triangular_solve | solution.py:40
  1098.5 70.3 %collective-permute-done.6 = f32[384,2304]{1,0:T(8,128)} collective-permute-done((f32[384,2304]{1,0:T(8,128)}, f32[384,2304]{1,0:T(8,128)}, u32[]{:S(2)}, u32[]{:S(2)}) %collective-permute-start.6) | collective-permute-done | bytes 3538976 | tf_op jit(solution)/shard_map/ppermute | solution.py:17
  1186.4 52.5 %collective-permute-done.7 = f32[384,768]{0,1:T(8,128)S(1)} collective-permute-done((f32[384,768]{0,1:T(8,128)S(1)}, f32[384,768]{0,1:T(8,128)S(1)}, u32[]{:S(2)}, u32[]{:S(2)}) %collective-permute-start.7) | collective-permute-done | bytes 1179680 | tf_op jit(solution)/shard_map/ppermute | solution.py:17
  1253.3 41.1 %collective-permute-done.8 = f32[768,768]{0,1:T(8,128)} collective-permute-done((f32[768,768]{0,1:T(8,128)}, f32[768,768]{0,1:T(8,128)}, u32[]{:S(2)}, u32[]{:S(2)}) %collective-permute-start.8) | collective-permute-done | bytes 2359328 | tf_op jit(solution)/shard_map/ppermute | solution.py:17
  1296.8 7.5 fusion.34
  (295 shorter events, 263.8 us)
Async XLA Ops:
  0.6 49.1 %copy-start = (s32[4,4,12,6]{2,1,3,0:T(4,128)S(1)}, s32[4,4,12,6]{2,1,3,0:T(4,128)}, u32[]{:S(2)}) copy-start(s32[4,4,12,6]{2,1,3,0:T(4,128)} %param.19) | copy-start | bytes 13828
  0.6 236.8 %collective-permute-start.1 = (f32[1024,1024]{1,0:T(8,128)}, f32[1024,1024]{1,0:T(8,128)}, u32[]{:S(2)}, u32[]{:S(2)}) collective-permute-start(f32[1024,1024]{1,0:T(8,128)} %bitcast.320), channel_id=1, source_target_pairs={{0,16},{4,20},{8,24},{12,28},{16,0},{20,4},{24,8},{28,12},{1,17},{... | collective-permute-start | bytes 12582920 | tf_op jit(solution)/shard_map/ppermute | solution.py:17
  7.4 228.7 %collective-permute-start = (f32[384,768]{0,1:T(8,128)}, f32[384,768]{0,1:T(8,128)}, u32[]{:S(2)}, u32[]{:S(2)}) collective-permute-start(f32[384,768]{0,1:T(8,128)} %bitcast), channel_id=1, source_target_pairs={{0,16},{4,20},{8,24},{12,28},{16,0},{20,4},{24,8},{28,12},{1,17},{... | collective-permute-start | bytes 3538952 | tf_op jit(solution)/shard_map/ppermute | solution.py:17
  237.4 1.4 copy-start.9
  278.8 7.2 copy-start.7
  278.8 7.8 copy-start.8
  278.8 8.5 copy-start.10
  287.3 3.7 copy-start.2
  295.0 1.4 copy-start.12
  439.1 79.8 %copy-start.11 = (f32[768,768]{0,1:T(8,128)S(1)}, f32[768,768]{0,1:T(8,128)}, u32[]{:S(2)}) copy-start(f32[768,768]{0,1:T(8,128)} %get-tuple-element.146) | copy-start | bytes 7077892
  516.5 9.8 copy-start.16
  529.6 7.0 copy-start.15
  531.8 111.7 %slice-start = ((s8[7077888]{0:T(1024)(128)(4,1)}), s8[2883584]{0:T(1024)(128)(4,1)S(1)}, s32[]{:S(2)}) async-start(s8[7077888]{0:T(1024)(128)(4,1)} %bitcast.304), calls=%async_computation | async-start | bytes 5767168
  536.6 104.2 %collective-permute-start.2 = (f32[768,768]{0,1:T(8,128)}, f32[768,768]{0,1:T(8,128)}, u32[]{:S(2)}, u32[]{:S(2)}) collective-permute-start(f32[768,768]{0,1:T(8,128)} %convolution_dynamic-update-slice_fusion), channel_id=1, source_target_pairs={{0,16},{4,20},{8,24},{12,28},{16,0},{20,4},{24,8},{28,12},{1,17},{... | collective-permute-start | bytes 7077896 | tf_op jit(solution)/shard_map/ppermute | solution.py:17
  539.2 104.3 %slice-start.1 = ((s8[7077888]{0:T(1024)(128)(4,1)}), s8[4194304]{0:T(1024)(128)(4,1)S(1)}, s32[]{:S(2)}) async-start(s8[7077888]{0:T(1024)(128)(4,1)} %bitcast.304), calls=%async_computation.1 | async-start | bytes 8388608
  692.2 2.1 copy-start.14
  702.1 51.7 %collective-permute-start.3 = (f32[768,768]{0,1:T(8,128)S(1)}, f32[768,768]{0,1:T(8,128)}, u32[]{:S(2)}, u32[]{:S(2)}) collective-permute-start(f32[768,768]{0,1:T(8,128)S(1)} %add.233), channel_id=1, source_target_pairs={{0,2},{1,3},{2,0},{3,1},{4,6},{5,7},{6,4},{7,5},{8,10},{9,11},{10,... | collective-permute-start | bytes 7077896 | tf_op jit(solution)/shard_map/ppermute | solution.py:17
  757.1 7.1 copy-start.17
  757.1 102.4 %collective-permute-start.4 = (f32[768,768]{0,1:T(8,128)}, f32[768,768]{0,1:T(8,128)}, u32[]{:S(2)}, u32[]{:S(2)}) collective-permute-start(f32[768,768]{0,1:T(8,128)} %add.234), channel_id=1, source_target_pairs={{0,16},{4,20},{8,24},{12,28},{16,0},{20,4},{24,8},{28,12},{1,17},{... | collective-permute-start | bytes 7077896 | tf_op jit(solution)/shard_map/ppermute | solution.py:17
  763.9 242.3 %collective-permute-start.5 = (f32[768,2304]{1,0:T(8,128)}, f32[768,2304]{1,0:T(8,128)}, u32[]{:S(2)}, u32[]{:S(2)}) collective-permute-start(f32[768,2304]{1,0:T(8,128)} %dynamic-slice_bitcast_fusion), channel_id=1, source_target_pairs={{0,2},{1,3},{2,0},{3,1},{4,6},{5,7},{6,4},{7,5},{8,10},{9,11},{10,... | collective-permute-start | bytes 21233672 | tf_op jit(solution)/shard_map/ppermute | solution.py:17
  866.5 1.4 copy-start.13
  1012.1 4.0 copy-start.3
  1016.1 152.7 %collective-permute-start.6 = (f32[384,2304]{1,0:T(8,128)}, f32[384,2304]{1,0:T(8,128)}, u32[]{:S(2)}, u32[]{:S(2)}) collective-permute-start(f32[384,2304]{1,0:T(8,128)} %dynamic-slice_bitcast_fusion.1), channel_id=1, source_target_pairs={{0,16},{4,20},{8,24},{12,28},{16,0},{20,4},{24,8},{28,12},{1,17},{... | collective-permute-start | bytes 10616840 | tf_op jit(solution)/shard_map/ppermute | solution.py:17
  1173.5 2.4 copy-start.4
  1186.3 52.6 %collective-permute-start.7 = (f32[384,768]{0,1:T(8,128)S(1)}, f32[384,768]{0,1:T(8,128)S(1)}, u32[]{:S(2)}, u32[]{:S(2)}) collective-permute-start(f32[384,768]{0,1:T(8,128)S(1)} %convolution_dynamic-update-slice_fusion.3), channel_id=1, source_target_pairs={{0,16},{4,20},{8,24},{12,28},{16,0},{20,4},{24,8},{28,12},{1,17},{... | collective-permute-start | bytes 3538952 | tf_op jit(solution)/shard_map/ppermute | solution.py:17
  1239.2 1.8 copy-start.6
  1241.0 53.4 %collective-permute-start.8 = (f32[768,768]{0,1:T(8,128)}, f32[768,768]{0,1:T(8,128)}, u32[]{:S(2)}, u32[]{:S(2)}) collective-permute-start(f32[768,768]{0,1:T(8,128)} %pad_maximum_fusion), channel_id=1, source_target_pairs={{0,2},{1,3},{2,0},{3,1},{4,6},{5,7},{6,4},{7,5},{8,10},{9,11},{10,... | collective-permute-start | bytes 7077896 | tf_op jit(solution)/shard_map/ppermute | solution.py:17
  1253.3 43.5 %copy-start.5 = (f32[384,2304]{1,0:T(8,128)S(1)}, f32[384,2304]{1,0:T(8,128)}, u32[]{:S(2)}) copy-start(f32[384,2304]{1,0:T(8,128)} %copy-done.4) | copy-start | bytes 10616836
  1296.8 7.5 copy-start.1
where the time goes:
time: 1320 us; the launch traced here: 1300 us
  waiting for transfers between devices  529 us (40%)
  other arithmetic  416 us (32%)
  local copies, waits for them, and re-layouts  186 us (14%)
  matrix products  159 us (12%)
    ppermute x9, waiting for transfers between devices, partner(): lax.ppermute(array, axis, [(i, i ^ 1 << apart) for i in range(lax.axis_si...  529 us
    another operation x45, other arithmetic, factor(): factor_lower = jnp.linalg.cholesky(pivot_block)  247 us
    another operation x5, other arithmetic, factor(): lax.linalg.triangular_solve(factor_lower, coupling, left_side=False, lowe...  123 us
    unnamed x60, local copies, waits for them, and re-layouts  48.8 us
    dot_general x6, matrix products, spread(): jnp.einsum('ia,ixky->axky', row_onehot, blocks, precision=HIGHEST_MODE)  36.9 us
    another operation x61, local copies, waits for them, and re-layouts  35.9 us
    another operation x22, matrix products, factor(): lax.linalg.triangular_solve(factor_lower, coupling, left_side=False, lowe...  32.7 us
    dot_general x6, matrix products, spread(): jnp.einsum('axky,kb->axby', placed, col_onehot, precision=HIGHEST_MODE)  32.3 us
  transfers between devices with their start and end apart: 9, of which 7 were waited for; matrix products, arithmetic and copies ran while one was open for 28% of the time, Pallas kernels for 0%

commit v1 on v0

v1 whole, which is shorter than its diff:
```python
import jax
import jax.numpy as jnp
import numpy as np
from jax import lax
from jax.experimental import pallas as pl
from jax.experimental.pallas import tpu as pltpu
from jax.sharding import PartitionSpec as P

TILE = 128
HALF = TILE // 2
CT = 8
P1T = 6
U1T = 12
P2T = 6
U2T = 12
ROWS = 8

HALF_U = U1T // 2
QUARTER = U2T // 4
PIVOT = P1T * TILE
SECOND = P2T * TILE

TRI_C = [(a, b) for a in range(CT) for b in range(a + 1)]
TRI_U = [(a, b) for a in range(HALF_U) for b in range(a + 1)]
TRI_P = [(a, b) for a in range(P1T // 2) for b in range(a + 1)]
N_OFF = (P1T // 2) ** 2
N_PIV = P1T * P1T
N_COUP = HALF_U * P1T
N_TRI = len(TRI_U)
N_CROSS = HALF_U * HALF_U
S_COUP = N_PIV
S_OWN = S_COUP + N_COUP
S_FAR = S_OWN + N_TRI
S_CROSS = S_FAR + N_COUP
S_OTH = S_CROSS + N_CROSS
N_FRONT = S_OTH + N_TRI
G_COUP = P2T * P2T
G_TRAIL = G_COUP + U2T * P2T
G_NONE = G_TRAIL + QUARTER * U2T

NT = (((1,), (1,)), ((), ()))
NN = (((1,), (0,)), ((), ()))
F32 = jnp.float32


def split(x):
    high = x.astype(jnp.bfloat16)
    return high, (x - high.astype(F32)).astype(jnp.bfloat16)


def dot3(a, b, dims):
    def one(p, q):
        return lax.dot_general(p, q, dims, preferred_element_type=F32)

    return one(a[0], b[0]) + (one(a[0], b[1]) + one(a[1], b[0]))


def mul(a, b, dims):
    return dot3(split(a), split(b), dims)


def factor_half(block, width):
    groups = HALF // ROWS
    sub = lax.broadcasted_iota(jnp.int32, (ROWS, TILE), 0)
    lane = lax.broadcasted_iota(jnp.int32, (ROWS, TILE), 1)

    def full(x):
        return jnp.broadcast_to(x, (ROWS, TILE))

    wide = jnp.concatenate([block, jnp.zeros((HALF, HALF), F32)], axis=1)
    a = [
        jnp.where(lane == sub + ROWS * g + HALF, 1.0, wide[ROWS * g : ROWS * g + ROWS])
        for g in range(groups)
    ]
    rows = [None] * HALF
    for j in range(0, HALF, width):
        gj, o = j // ROWS, j % ROWS
        cols = {g: [full(a[g][:, j + i : j + i + 1]) for i in range(width)] for g in range(gj, groups)}
        s = [
            [full(cols[gj][k][o + i : o + i + 1, :]) if k <= i else None for k in range(width)]
            for i in range(width)
        ]
        u = [full(a[gj][o + i : o + i + 1, :]) for i in range(width)]
        inv = [None] * width
        low = [[None] * width for _ in range(width)]
        for k in range(width):
            inv[k] = 1.0 / s[k][k]
            for i in range(k + 1, width):
                low[i][k] = s[i][k] * inv[k]
            for i in range(k + 1, width):
                for q in range(k + 1, i + 1):
                    s[i][q] = s[i][q] - low[i][k] * s[q][k]
        for i in range(width):
            for k in range(i):
                u[i] = u[i] - low[i][k] * u[k]
            rows[j + i] = u[i] * lax.rsqrt(s[i][i])
        scaled = [u[i] * inv[i] for i in range(width)]
        for g in range(gj if o + width < ROWS else gj + 1, groups):
            c = cols[g]
            for i in range(width):
                for k in range(i):
                    c[i] = c[i] - c[k] * low[i][k]
            for i in range(width):
                a[g] = a[g] - c[i] * scaled[i]
    out = []
    for g in range(groups):
        v = rows[ROWS * g]
        for i in range(1, ROWS):
            v = jnp.where(sub == i, rows[ROWS * g + i], v)
        out.append(v)
    both = jnp.concatenate(out, axis=0)
    return both[:, :HALF], both[:, HALF:]


def factor(a, low, inv, tiles, width):
    d = a[0:TILE, 0:TILE]
    zero = jnp.zeros((HALF, HALF), F32)
    ri = lax.broadcasted_iota(jnp.int32, (HALF, HALF), 0)
    ci = lax.broadcasted_iota(jnp.int32, (HALF, HALF), 1)
    for k in range(tiles):
        k0, k1, k2 = k * TILE, (k + 1) * TILE, (k + 2) * TILE
        u1, w1 = factor_half(d[:HALF, :HALF], width)
        l21 = mul(d[HALF:, :HALF], w1, NT)
        u2, w2 = factor_half(d[HALF:, HALF:] - mul(l21, l21, NT), width)
        w21 = -mul(w2, mul(l21, w1, NN), NN)
        w = jnp.concatenate([jnp.concatenate([w1, zero], 1), jnp.concatenate([w21, w2], 1)], 0)
        ws = split(w)
        inv[k0:k1, k0:k1] = w
        if k + 1 < tiles:
            p = dot3(split(a[k1:k2, k0:k1]), ws, NT)
            low[k1:k2, k0:k1] = p
            ps = split(p)
            d = a[k1:k2, k1:k2] - dot3(ps, ps, NT)
        l1 = jnp.where(ri >= ci, u1.T, 0.0)
        l2 = jnp.where(ri >= ci, u2.T, 0.0)
        low[k0:k1, k0:k1] = jnp.concatenate(
            [jnp.concatenate([l1, zero], 1), jnp.concatenate([l21, l2], 1)], 0
        )
        if k + 2 < tiles:
            low[k2:, k0:k1] = dot3(split(a[k2:, k0:k1]), ws, NT)
            for j in range(k + 1, tiles):
                j0 = j * TILE
                top = max(j0, k2)
                a[top:, j0 : j0 + TILE] = a[top:, j0 : j0 + TILE] - mul(
                    low[top:, k0:k1], low[j0 : j0 + TILE, k0:k1], NT
                )
        if k > 0:
            x = mul(low[k0:k1, 0:k0], inv[0:k0, 0:k0], NN)
            inv[k0:k1, 0:k0] = -dot3(ws, split(x), NN)
        if k + 1 < tiles:
            rest = jnp.zeros((TILE, (tiles - k - 1) * TILE), F32)
            low[k0:k1, k1:] = rest
            inv[k0:k1, k1:] = rest


def padded(a, tile_of, live, tiles):
    ri = lax.broadcasted_iota(jnp.int32, (TILE, TILE), 0)
    ci = lax.broadcasted_iota(jnp.int32, (TILE, TILE), 1)
    eye = jnp.where(ri == ci, 1.0, 0.0)
    for i in range(tiles):
        kept = (jnp.int32(i) < live).astype(F32)
        for j in range(i + 1):
            value = tile_of(i, j) * kept
            if i == j:
                value = value + eye * (1.0 - kept)
            a[i * TILE : (i + 1) * TILE, j * TILE : (j + 1) * TILE] = value


def copy_all(pairs, sems):
    copies = [pltpu.make_async_copy(src, dst, sems.at[n]) for n, (src, dst) in enumerate(pairs)]
    for c in copies:
        c.start()
    for c in copies:
        c.wait()


def tile_at(ref, row, col):
    return ref.at[
        pl.ds(pl.multiple_of(row * TILE, TILE), TILE), pl.ds(pl.multiple_of(col * TILE, TILE), TILE)
    ]


def pack_first(tab, block, pivot, out, sems):
    side = tab[CT]
    pairs = []
    for n, (a, b) in enumerate(TRI_C):
        pairs.append((tile_at(block, tab[a], tab[b]), out.at[n]))
    for n, (a, b) in enumerate(TRI_P):
        pairs.append((tile_at(pivot, a, side * (P1T // 2) + b), out.at[len(TRI_C) + n]))
    copy_all(pairs, sems)


def pack_rest(tab, block, pivot, rows, second, coup, own, kept, cross, off, coup_two, sems):
    side = tab[CT]
    order = CT + 1
    local = order + CT
    pairs = []
    for r in range(HALF_U):
        row = tab[local + r] - side * HALF_U
        for c in range(P1T):
            pairs.append((tile_at(rows, row, c), coup.at[r * P1T + c]))
    for n, (a, b) in enumerate(TRI_U):
        row = tab[local + a] - side * HALF_U
        pairs.append((tile_at(rows, row, P1T + tab[local + b]), own.at[n]))
    for n, (a, b) in enumerate(TRI_C):
        pairs.append((tile_at(block, tab[order + a], tab[order + b]), kept.at[n]))
    for i in range(HALF_U):
        row = tab[local + i] - side * HALF_U
        for k in range(HALF_U):
            pairs.append(
                (tile_at(rows, row, P1T + tab[local + HALF_U + k]), cross.at[i * HALF_U + k])
            )
    for i in range(P1T // 2):
        for k in range(P1T // 2):
            pairs.append(
                (tile_at(pivot, i, (1 - side) * (P1T // 2) + k), off.at[i * (P1T // 2) + k])
            )
    for n, (i, k) in enumerate(TRI_P):
        pairs.append((tile_at(pivot, i, side * (P1T // 2) + k), off.at[N_OFF + n]))
    for r in range(QUARTER):
        for c in range(P2T):
            pairs.append((tile_at(second, r, c), coup_two.at[r * P2T + c]))
    copy_all(pairs, sems)


T_SIDE = 0
T_LIVE = 1
T_LOCAL = 2
T_FILL = T_LOCAL + U1T
T_SLOT = T_FILL + U1T * P1T
T_SLOT_FAR = T_SLOT + len(TRI_C)


def panel_rows(tile_of, count, live, inv, put):
    parts = split(inv)
    for r in range(0, count, 2):
        block = jnp.concatenate(
            [
                jnp.concatenate([tile_of(r + i, c) for c in range(P1T)], axis=1)
                for i in range(2)
            ],
            axis=0,
        )
        lane = lax.broadcasted_iota(jnp.int32, block.shape, 1)
        block = jnp.where(lane < live * TILE, block, 0.0)
        put(r, dot3(split(block), parts, NT))


def first_kernel(
    tab, mine, theirs, coup, own, cross, off,
    lower_out, inv_out, panel_out, rows_out, own_out, far_out,
    front, a, low, sem,
):
    side = tab[T_SIDE]
    live = tab[T_LIVE]
    half = P1T // 2
    front[0:N_PIV] = jnp.zeros((N_PIV, TILE, TILE), F32)
    for n, (i, k) in enumerate(TRI_P):
        front[(side * half + i) * P1T + side * half + k] = off[N_OFF + n]
        front[((1 - side) * half + i) * P1T + (1 - side) * half + k] = theirs[len(TRI_C) + n]
    for i in range(half):
        for k in range(half):

            @pl.when(side == 0)
            def _():
                front[(half + k) * P1T + i] = off[i * half + k].T

            @pl.when(side != 0)
            def _():
                front[(half + i) * P1T + k] = off[i * half + k]

    def scale(n, carry):
        front[S_COUP + n] = coup[n] * tab[T_FILL + n].astype(F32)
        front[S_FAR + n] = jnp.zeros((TILE, TILE), F32)
        front[S_CROSS + n] = cross[n]
        return carry

    lax.fori_loop(0, N_COUP, scale, 0)

    def copy(n, carry):
        front[S_OWN + n] = own[n]
        front[S_OTH + n] = jnp.zeros((TILE, TILE), F32)
        return carry

    lax.fori_loop(0, N_TRI, copy, 0)

    def extend(n, carry):
        here = tab[T_SLOT + n]
        front[here] = front[here] + mine[n]
        there = tab[T_SLOT_FAR + n]
        front[there] = front[there] + theirs[n]
        return carry

    lax.fori_loop(0, len(TRI_C), extend, 0)
    leave = pltpu.make_async_copy(front.at[pl.ds(S_FAR, N_FRONT - S_FAR)], far_out, sem)
    leave.start()
    padded(a, lambda i, j: front[i * P1T + j], live, P1T)
    factor(a, low, inv_out, P1T, 4)
    lower_out[...] = low[pl.ds(pl.multiple_of(side * (PIVOT // 2), TILE), PIVOT // 2), :]

    def put(r, rows):
        panel_out[r * TILE : (r + 2) * TILE, :] = rows
        for i in range(2):
            place = tab[T_LOCAL + r + i] - side * HALF_U
            rows_out[pl.ds(pl.multiple_of(place * TILE, TILE), TILE), :] = rows[
                i * TILE : (i + 1) * TILE
            ]

    panel_rows(lambda r, c: front[S_COUP + r * P1T + c], HALF_U, live, inv_out[...], put)
    for i in range(HALF_U):
        left = split(panel_out[i * TILE : (i + 1) * TILE, :])
        product = dot3(left, split(panel_out[0 : (i + 1) * TILE, :]), NT)
        for k in range(i + 1):
            n = i * (i + 1) // 2 + k
            own_out[n] = front[S_OWN + n] - product[:, k * TILE : (k + 1) * TILE]
    leave.wait()


def second_kernel(tab, far, coup, inv, panel, cross_out, oth_out, panel_far):
    live = tab[T_LIVE]

    def tile_of(r, c):
        n = r * P1T + c
        return far[n] + coup[n] * tab[T_FILL + N_COUP + n].astype(F32)

    def put(r, rows):
        panel_far[r * TILE : (r + 2) * TILE, :] = rows

    panel_rows(tile_of, HALF_U, live, inv[...], put)
    right = split(panel_far[...])
    for i in range(0, HALF_U, 2):
        product = dot3(split(panel[i * TILE : (i + 2) * TILE, :]), right, NT)
        for q in range(2):
            for k in range(HALF_U):
                n = (i + q) * HALF_U + k
                cross_out[n] = (
                    far[N_COUP + n]
                    - product[q * TILE : (q + 1) * TILE, k * TILE : (k + 1) * TILE]
                )
    for i in range(HALF_U):
        left = split(panel_far[i * TILE : (i + 1) * TILE, :])
        product = dot3(left, split(panel_far[0 : (i + 1) * TILE, :]), NT)
        for k in range(i + 1):
            n = i * (i + 1) // 2 + k
            oth_out[n] = far[N_COUP + N_CROSS + n] - product[:, k * TILE : (k + 1) * TILE]


Q_LIVE = 0
Q_MINE = 1
Q_FILL = 5
Q_DIRECT = Q_FILL + U2T * P2T
N_S1 = 2 * N_TRI + N_CROSS
Q_TURNED = Q_DIRECT + 2 * N_S1


def third_kernel(
    tab, own0, cross0, oth0, own1, cross1, oth1, piv0, piv1, piv2, piv3, second,
    lower_out, inv_out, g_out,
    g, a, low, sem,
):
    units = SECOND // 4 // HALF
    for s, piv in enumerate((piv0, piv1, piv2, piv3)):
        for i in range(units):
            unit = tab[Q_MINE + s] * units + i
            row = unit // 2
            start = pl.multiple_of((unit % 2) * HALF, HALF)
            for c in range(P2T):
                g[row * P2T + c, pl.ds(start, HALF), :] = piv[
                    i * HALF : (i + 1) * HALF, c * TILE : (c + 1) * TILE
                ]

    def clear(n, carry):
        g[G_COUP + n] = jnp.zeros((TILE, TILE), F32)
        return carry

    lax.fori_loop(0, U2T * P2T, clear, 0)
    for r in range(QUARTER):
        for c in range(U2T):
            g[G_TRAIL + r * U2T + c] = second[
                r * TILE : (r + 1) * TILE, SECOND + c * TILE : SECOND + (c + 1) * TILE
            ]
    first = 0
    for ref in (own0, cross0, oth0, own1, cross1, oth1):

        def extend(n, carry, ref=ref, first=first):
            direct = tab[Q_DIRECT + first + n]
            turned = tab[Q_TURNED + first + n]
            g[direct] = g[direct] + ref[n]

            @pl.when(turned != G_NONE)
            def _():
                g[turned] = g[turned] + ref[n].T

            return carry

        lax.fori_loop(0, ref.shape[0], extend, 0)
        first += ref.shape[0]
    leave = pltpu.make_async_copy(g.at[pl.ds(G_COUP, G_NONE - G_COUP)], g_out, sem)
    leave.start()
    padded(a, lambda i, j: g[i * P2T + j], tab[Q_LIVE], P2T)
    factor(a, low, inv_out, P2T, 8)
    start = tab[Q_MINE] * (SECOND // 4)
    lower_out[...] = low[pl.ds(pl.multiple_of(start, HALF), SECOND // 4), :]
    leave.wait()


def last_kernel(tab, g, inv, coup0, coup1, coup2, coup3, panel_out, schur_out, panels):
    live = tab[Q_LIVE]
    parts = split(inv[...])
    for s, coup in enumerate((coup0, coup1, coup2, coup3)):
        quarter = tab[Q_MINE + s]
        rows = []
        for r in range(QUARTER):
            row = quarter * QUARTER + r
            rows.append(
                jnp.concatenate(
                    [
                        g[row * P2T + c]
                        + coup[r * P2T + c] * tab[Q_FILL + row * P2T + c].astype(F32)
                        for c in range(P2T)
                    ],
                    axis=1,
                )
            )
        block = jnp.concatenate(rows, axis=0)
        lane = lax.broadcasted_iota(jnp.int32, block.shape, 1)
        block = jnp.where(lane < live * TILE, block, 0.0)
        panel = dot3(split(block), parts, NT)
        panels[quarter] = panel
        if s == 0:
            panel_out[...] = panel
    left = split(panel_out[...])
    wide = QUARTER * TILE
    for q in range(4):
        product = dot3(left, split(panels[q]), NT)
        for r in range(QUARTER):
            for c in range(QUARTER):
                col = q * QUARTER + c
                schur_out[r * TILE : (r + 1) * TILE, col * TILE : (col + 1) * TILE] = (
                    g[G_TRAIL - G_COUP + r * U2T + col]
                    - product[r * TILE : (r + 1) * TILE, c * TILE : (c + 1) * TILE]
                )


def swap(array, axis):
    size = lax.axis_size(axis)
    return lax.ppermute(array, axis, [(i, i ^ (size // 2)) for i in range(size)])


def tiles(count):
    return jax.ShapeDtypeStruct((count, TILE, TILE), F32)


def dense(rows, cols):
    return jax.ShapeDtypeStruct((rows, cols), F32)


SMEM = pl.BlockSpec(memory_space=pltpu.SMEM)
VMEM = pl.BlockSpec(memory_space=pltpu.VMEM)
HBM = pl.BlockSpec(memory_space=pl.ANY)
LIMIT = 56 << 20


def cost(flops, count):
    return pl.CostEstimate(flops=flops, bytes_accessed=count * TILE * TILE * 4, transcendentals=0)


def tri(i, k):
    return i * (i + 1) // 2 + k


def local_order(second_map, side):
    unit = jnp.arange(U1T, dtype=jnp.int32)
    rank = second_map + jnp.where(unit // HALF_U == side, 0, P2T + U2T)
    place = jnp.sum((rank[None, :] < rank[:, None]).astype(jnp.int32), axis=1)
    hit = (place[None, :] == unit[:, None]).astype(jnp.int32)
    return place, hit


def place_of(child_map, place):
    unit = jnp.arange(U1T, dtype=jnp.int32)
    hit = (child_map[:, None] - P1T == unit[None, :]).astype(jnp.int32)
    return jnp.where(child_map < P1T, child_map, P1T + jnp.sum(hit * place[None, :], axis=1))


def sort_by(key):
    spot = jnp.sum((key[None, :] < key[:, None]).astype(jnp.int32), axis=1)
    hit = (spot[None, :] == jnp.arange(CT, dtype=jnp.int32)[:, None]).astype(jnp.int32)
    order = jnp.sum(hit * jnp.arange(CT, dtype=jnp.int32)[None, :], axis=1)
    return order, jnp.sum(hit * key[None, :], axis=1)


def turned_key(key):
    return jnp.where(key < P1T, key, P1T + (key - P1T + HALF_U) % U1T)


def slots(keys):
    row = keys[np.array([a for a, b in TRI_C])]
    col = keys[np.array([b for a, b in TRI_C])]
    own = P1T + HALF_U
    pivot = row * P1T + col
    coup = jnp.where(row >= own, S_COUP + (row - own) * P1T, S_FAR + (row - P1T) * P1T) + col
    near = S_OWN + tri(row - own, col - own)
    cross = S_CROSS + (row - own) * HALF_U + col - P1T
    other = S_OTH + tri(row - P1T, col - P1T)
    rest = jnp.where(row < own, other, jnp.where(col < own, cross, near))
    return jnp.where(row < P1T, pivot, jnp.where(col < P1T, coup, rest))


PAIRS = (
    TRI_U
    + [(i, HALF_U + k) for i in range(HALF_U) for k in range(HALF_U)]
    + [(HALF_U + i, HALF_U + k) for i, k in TRI_U]
)


def targets(goal, quarter):
    row = goal[np.array([a for a, b in PAIRS])]
    col = goal[np.array([b for a, b in PAIRS])]

    def index(r, c):
        mine = (r - P2T) // QUARTER == quarter
        coup = G_COUP + (r - P2T) * P2T + c
        trail = G_TRAIL + (r - P2T - quarter * QUARTER) * U2T + c - P2T
        rest = jnp.where(c < P2T, coup, jnp.where(mine, trail, G_NONE))
        return jnp.where(r < P2T, jnp.where((c < P2T) & (r >= c), r * P2T + c, G_NONE), rest)

    direct = index(row, col)
    return direct, jnp.where(row == col, G_NONE, index(col, row))


def body(
    contribution,
    pivot_one,
    rows_one,
    pivot_two,
    rows_two,
    map_one,
    map_two,
    fill_one,
    fill_two,
    live_one,
    live_two,
):
    size_lo = lax.axis_size("lo")
    size_hi = lax.axis_size("hi")
    half_lo = size_lo // 2
    half_hi = size_hi // 2
    index_lo = lax.axis_index("lo")
    index_hi = lax.axis_index("hi")
    side_lo = index_lo // half_lo
    side_hi = index_hi // half_hi
    front_lo = index_lo % half_lo
    front_hi = index_hi % half_hi
    far_lo = (index_lo + half_lo) % size_lo
    far_hi = (index_hi + half_hi) % size_hi
    block, pivot, rows = contribution[0, 0], pivot_one[0, 0], rows_one[0, 0]
    pivot_second, rows_second = pivot_two[0, 0], rows_two[0, 0]
    params = pltpu.CompilerParams(vmem_limit_bytes=LIMIT)

    second_map = map_two[index_hi, front_lo]
    place, hit = local_order(second_map, side_lo)
    key = place_of(map_one[index_hi, index_lo], place)
    order_sent, _ = sort_by(key)
    tab_first = jnp.concatenate([order_sent, side_lo[None]]).astype(jnp.int32)
    n_first = len(TRI_C) + len(TRI_P)
    sent = pl.pallas_call(
        pack_first,
        out_shape=tiles(n_first),
        in_specs=[SMEM, HBM, HBM],
        out_specs=HBM,
        scratch_shapes=[pltpu.SemaphoreType.DMA((n_first,))],
        name="pack_first",
        compiler_params=params,
        cost_estimate=cost(0, 2 * n_first),
    )(tab_first, block, pivot)
    got_first = swap(sent, "lo")

    unit = jnp.arange(U1T, dtype=jnp.int32)
    local = jnp.sum(hit * unit[None, :], axis=1)
    order_kept, keys = sort_by(turned_key(key))
    tab_rest = jnp.concatenate([tab_first, order_kept, local]).astype(jnp.int32)
    shapes = [tiles(N_COUP), tiles(N_TRI), tiles(len(TRI_C)), tiles(N_CROSS), tiles(N_OFF + len(TRI_P)), tiles(QUARTER * P2T)]
    n_rest = sum(s.shape[0] for s in shapes)
    coup, own, kept, cross, off, coup_two = pl.pallas_call(
        pack_rest,
        out_shape=shapes,
        in_specs=[SMEM, HBM, HBM, HBM, HBM],
        out_specs=[HBM] * len(shapes),
        scratch_shapes=[pltpu.SemaphoreType.DMA((n_rest,))],
        name="pack_rest",
        compiler_params=params,
        cost_estimate=cost(0, 2 * n_rest),
    )(tab_rest, block, pivot, rows, rows_second)
    got_coup = swap(coup, "lo")
    got_own = swap(own, "lo")
    got_pivot = swap(pivot_second, "lo")
    got_two = swap(coup_two, "lo")

    far_key = place_of(map_one[index_hi, far_lo], place)
    _, far_keys = sort_by(turned_key(far_key))
    live_first = live_one[index_hi, front_lo]
    fill_first = jnp.sum(hit[:, :, None] * fill_one[index_hi, front_lo][None, :, :], axis=1)
    tab_one = jnp.concatenate(
        [side_lo[None], live_first[None], local, fill_first.reshape(-1), slots(keys), slots(far_keys)]
    ).astype(jnp.int32)
    mega = 2 * TILE**3
    half_rows = HALF_U * TILE
    lower_one, inv_one, panel_own, panel_one, s_own, far_part = pl.pallas_call(
        first_kernel,
        out_shape=[
            dense(PIVOT // 2, PIVOT), dense(PIVOT, PIVOT), dense(half_rows, PIVOT),
            dense(half_rows, PIVOT), tiles(N_TRI), tiles(N_FRONT - S_FAR),
        ],
        in_specs=[SMEM] + [VMEM] * 6,
        out_specs=[VMEM] * 5 + [HBM],
        scratch_shapes=[
            pltpu.VMEM((N_FRONT, TILE, TILE), F32),
            pltpu.VMEM((PIVOT, PIVOT), F32),
            pltpu.VMEM((PIVOT, PIVOT), F32),
            pltpu.SemaphoreType.DMA,
        ],
        name="first_front_own",
        compiler_params=params,
        cost_estimate=cost(4000 * mega, 2 * N_FRONT),
    )(tab_one, kept, got_first, coup, own, cross, off)
    s_own_far = swap(s_own, "hi")
    pivot_hi, got_pivot_hi = swap(pivot_second, "hi"), swap(got_pivot, "hi")
    two_hi = swap(coup_two, "hi")

    s_cross, s_part = pl.pallas_call(
        second_kernel,
        out_shape=[tiles(N_CROSS), tiles(N_TRI)],
        in_specs=[SMEM] + [VMEM] * 4,
        out_specs=[VMEM] * 2,
        scratch_shapes=[pltpu.VMEM((half_rows, PIVOT), F32)],
        name="first_front_other",
        compiler_params=params,
        cost_estimate=cost(1500 * mega, 300),
    )(tab_one, far_part, got_coup, inv_one, panel_own)
    s_cross_far = swap(s_cross, "hi")
    s_oth = s_part + got_own
    s_oth_far = swap(s_oth, "hi")
    two_both = swap(got_two, "hi")

    quarter = 2 * side_hi + side_lo
    _, hit_far = local_order(map_two[far_hi, front_lo], side_lo)
    goal = jnp.sum(hit * second_map[None, :], axis=1)
    goal_far = jnp.sum(hit_far * map_two[far_hi, front_lo][None, :], axis=1)
    direct, turned = targets(goal, quarter)
    direct_far, turned_far = targets(goal_far, quarter)
    fill_second = fill_two[front_hi, front_lo].reshape(-1)
    quarters = jnp.stack(
        [quarter, 2 * side_hi + 1 - side_lo, 2 * (1 - side_hi) + side_lo, 2 * (1 - side_hi) + 1 - side_lo]
    )
    tab_two = jnp.concatenate(
        [
            live_two[front_hi, front_lo][None], quarters, fill_second,
            direct, direct_far, turned, turned_far,
        ]
    ).astype(jnp.int32)
    lower_two, inv_two, gathered = pl.pallas_call(
        third_kernel,
        out_shape=[dense(SECOND // 4, SECOND), dense(SECOND, SECOND), tiles(G_NONE - G_COUP)],
        in_specs=[SMEM] + [VMEM] * 11,
        out_specs=[VMEM] * 2 + [HBM],
        scratch_shapes=[
            pltpu.VMEM((G_NONE + 1, TILE, TILE), F32),
            pltpu.VMEM((SECOND, SECOND), F32),
            pltpu.VMEM((SECOND, SECOND), F32),
            pltpu.SemaphoreType.DMA,
        ],
        name="second_front_pivot",
        compiler_params=params,
        cost_estimate=cost(4000 * mega, 2 * G_NONE),
    )(
        tab_two, s_own, s_cross, s_oth, s_own_far, s_cross_far, s_oth_far,
        pivot_second, got_pivot, pivot_hi, got_pivot_hi, rows_second,
    )
    quarter_rows = QUARTER * TILE
    panel_two, schur_two = pl.pallas_call(
        last_kernel,
        out_shape=[dense(quarter_rows, SECOND), dense(quarter_rows, U2T * TILE)],
        in_specs=[SMEM] + [VMEM] * 6,
        out_specs=[VMEM] * 2,
        scratch_shapes=[pltpu.VMEM((4, quarter_rows, SECOND), F32)],
        name="second_front_rows",
        compiler_params=params,
        cost_estimate=cost(1000 * mega, 300),
    )(tab_two, gathered, inv_two, coup_two, got_two, two_hi, two_both)
    return (
        lower_one[None, None],
        panel_one[None, None],
        lower_two[None, None],
        panel_two[None, None],
        schur_two[None, None],
    )


def solution(mesh):
    split_both = P("hi", "lo", None, None)
    return jax.shard_map(
        body,
        mesh=mesh,
        in_specs=(split_both,) * 5 + (P(),) * 6,
        out_specs=(split_both,) * 5,
        check_vma=False,
    )
```

time: 1320 us -> 782 us (0.59)
  Pallas kernels: 0 us -> 551 us
  other arithmetic: 416 us -> 21.9 us
  waiting for transfers between devices: 529 us -> 176 us
  local copies, waits for them, and re-layouts: 186 us -> 11.4 us
  matrix products: 159 us -> 0 us
    pallas_call x0 -> x6, Pallas kernels: none -> 551 us  [the longest x1 325 us: body(): pl.pallas_call(pack_rest, out_shape=shapes, in_specs=[SMEM, HBM, HBM, HBM...]
    another operation x50 -> x0, other arithmetic: 370 us -> none  [the longest x45 247 us: factor(): factor_lower = jnp.linalg.cholesky(pivot_block)]
    ppermute x9 -> x12, waiting for transfers between devices: 529 us -> 176 us  [swap(): return lax.ppermute(array, axis, [(i, i ^ size // 2) for i in range(size)])]
    dot_general x14 -> x0, matrix products: 102 us -> none  [the longest x6 36.9 us: spread(): jnp.einsum('ia,ixky->axky', row_onehot, blocks, precision=HIGHEST_MODE)]
    another operation x42 -> x0, matrix products: 56.6 us -> none  [the longest x22 32.7 us: factor(): lax.linalg.triangular_solve(factor_lower, coupling, left_side=False, lowe...]
    another operation x101 -> x1, local copies, waits for them, and re-layouts: 55.7 us -> 0.08 us  [body(): fill_second = fill_two[front_hi, front_lo].reshape(-1)]
    unnamed x60 -> x63, local copies, waits for them, and re-layouts: 48.8 us -> 1.41 us
    reshape x7 -> x1, local copies, waits for them, and re-layouts: 37.8 us -> 0.08 us  [body(): fill_first.reshape(-1)]
  transfers between devices with their start and end apart: 9 -> 12, of which waited for: 7 -> 6; matrix products, arithmetic and copies ran while one was open for 28% -> 4% of each run, Pallas kernels for 0% -> 58%
where the time goes in v1:
time: 782 us; the launch traced here: 778 us
  Pallas kernels  551 us (70%)
  waiting for transfers between devices  176 us (23%)
  other arithmetic  21.9 us (3%)
  starting transfers between devices  14.8 us (2%)
  local copies, waits for them, and re-layouts  11.4 us (1%)
    pallas_call x1, Pallas kernels, body(): pl.pallas_call(pack_rest, out_shape=shapes, in_specs=[SMEM, HBM, HBM, HBM...  325 us
    ppermute x12, waiting for transfers between devices, swap(): return lax.ppermute(array, axis, [(i, i ^ size // 2) for i in range(size)])  176 us
    pallas_call x1, Pallas kernels, body(): pl.pallas_call(pack_first, out_shape=tiles(n_first), in_specs=[SMEM, HBM,...  85.5 us
    pallas_call x1, Pallas kernels, body(): pl.pallas_call(first_kernel, out_shape=[dense(PIVOT // 2, PIVOT), dense(P...  58.6 us
    pallas_call x1, Pallas kernels, body(): pl.pallas_call(third_kernel, out_shape=[dense(SECOND // 4, SECOND), dense...  48 us
    pallas_call x1, Pallas kernels, body(): pl.pallas_call(last_kernel, out_shape=[dense(quarter_rows, SECOND), dense...  18.1 us
    pallas_call x1, Pallas kernels, body(): pl.pallas_call(second_kernel, out_shape=[tiles(N_CROSS), tiles(N_TRI)], i...  16.3 us
  transfers between devices with their start and end apart: 12, of which 6 were waited for; matrix products, arithmetic and copies ran while one was open for 4% of the time, Pallas kernels for 58%

profile of v1, /device:TPU:0, one launch (start us, length us, event | category | flops | bytes accessed | tf_op | source)
XLA Modules:
  0.0 777.6 jit_solution(2961668090072751250)
XLA Ops:
  0.7 0.7 fusion.23
  1.4 0.2 convert_reduce_fusion.1
  1.6 0.8 broadcast_add_fusion.1
  2.4 0.2 select_reduce_fusion.6
  2.6 0.8 compare_select_fusion.2
  3.4 0.2 convert_reduce_fusion.2
  3.7 0.6 pad_add_fusion.1.tab
  4.3 85.5 %pack_first.1 = f32[42,128,128]{2,1,0:T(8,128)} custom-call(s32[9]{0:T(128)} %pad_add_fusion.1.tab, f32[1024,1024]{1,0:T(8,128)} %bitcast.63, f32[384,768]{1,0:T(8,128)} %bitcast.66), custom_call_target="tpu_custom_call" | custom-call | bytes 5505024 | tf_op jit(solution)/shard_map/pack_first/pallas_call | solution.py:567
  89.8 4.1 collective-permute-start
  93.9 0.2 convert_reduce_fusion.4
  94.3 0.6 pad_add_fusion.tab
  94.9 325.0 %pack_rest.1 = (f32[36,128,128]{2,1,0:T(8,128)}, f32[21,128,128]{2,1,0:T(8,128)}, f32[36,128,128]{2,1,0:T(8,128)}, f32[36,128,128]{2,1,0:T(8,128)}, f32[15,128,128]{2,1,0:T(8,128)}, /*index=5*/f32[18,128,128]{2,1,0:T(8,128)}) custom-call(s32[29]{0:T(128)} %pad_add_fusion.tab, f32[1024,1024]{1,0:T(8,128)} %bitcast.64, f32[384,768]{1,0:T(8,128)} %bitcast.67, ...), custom_call_target="tpu_custom_call" | custom-call | bytes 21233664 | tf_op jit(solution)/shard_map/pack_rest/pallas_call | solution.py:585
  420.0 2.9 collective-permute-start.2
  422.9 0.8 gather_fusion
  423.7 0.8 gather_fusion.1
  424.5 0.2 convert_reduce_fusion.3
  424.8 0.8 gather_fusion.2
  425.6 0.8 gather_fusion.3
  426.4 0.7 constant_dynamic-slice_fusion.1
  427.1 0.3 multiply_reduce_fusion
  427.5 1.3 dynamic_slice.25
  428.8 1.3 concatenate.13.tab
  430.1 58.6 %first_front_own.1 = (f32[384,768]{1,0:T(8,128)}, f32[768,768]{1,0:T(8,128)}, f32[768,768]{1,0:T(8,128)}, f32[768,768]{1,0:T(8,128)}, f32[21,128,128]{2,1,0:T(8,128)}, /*index=5*/f32[93,128,128]{2,1,0:T(8,128)}) custom-call(s32[158]{0:T(256)} %concatenate.13.tab, f32[36,128,128]{2,1,0:T(8,128)} %get-tuple-element.24.mine, ...), custom_call_target="tpu_custom_call" | custom-call | flops 16777216000 | bytes 24379392 | tf_op jit(solution)/shard_map/first_front_own/pallas_call | solution.py:609
  488.7 66.4 %collective-permute-done.1.coup = f32[36,128,128]{2,1,0:T(8,128)} collective-permute-done((f32[36,128,128]{2,1,0:T(8,128)}, f32[36,128,128]{2,1,0:T(8,128)}, u32[]{:S(2)}, u32[]{:S(2)}) %collective-permute-start.1) | collective-permute-done | bytes 2359328 | tf_op jit(solution)/shard_map/ppermute | solution.py:447
  555.1 16.3 %first_front_other.1 = (f32[36,128,128]{2,1,0:T(8,128)}, f32[21,128,128]{2,1,0:T(8,128)}) custom-call(s32[158]{0:T(256)} %concatenate.13.tab, f32[93,128,128]{2,1,0:T(8,128)} %get-tuple-element.32.far, f32[36,128,128]{2,1,0:T(8,128)} %collective-permute-done.1.coup, f32[768,768]{1,0:T(8,128)} %get-tuple-element.33.inv, f32[768,768]{1,0:T(8,128)} %get-tuple-element.34.panel), custom_call_target="tpu_custom_call" | custom-call | flops 6291456000 | bytes 19660800 | tf_op jit(solution)/shard_map/first_front_other/pallas_call | solution.py:631
  571.6 1.6 collective-permute-start.4
  573.2 0.5 collective-permute-start.7
  573.7 23.4 %collective-permute-done.2 = f32[21,128,128]{2,1,0:T(8,128)S(1)} collective-permute-done((f32[21,128,128]{2,1,0:T(8,128)}, f32[21,128,128]{2,1,0:T(8,128)S(1)}, u32[]{:S(2)}, u32[]{:S(2)}) %collective-permute-start.2) | collective-permute-done | bytes 1376288 | tf_op jit(solution)/shard_map/ppermute | solution.py:447
  597.2 1.5 add.498.oth0
  598.6 1.6 collective-permute-start.5
  600.2 0.5 collective-permute-start.3
  600.7 8.0 %collective-permute-done.6.piv1 = f32[192,768]{1,0:T(8,128)} collective-permute-done((f32[192,768]{1,0:T(8,128)S(1)}, f32[192,768]{1,0:T(8,128)}, u32[]{:S(2)}, u32[]{:S(2)}) %collective-permute-start.6) | collective-permute-done | bytes 589856 | tf_op jit(solution)/shard_map/ppermute | solution.py:447
  609.0 0.7 fusion.27
  609.7 29.1 %collective-permute-done.7.piv2 = f32[192,768]{1,0:T(8,128)} collective-permute-done((f32[192,768]{1,0:T(8,128)S(1)}, f32[192,768]{1,0:T(8,128)}, u32[]{:S(2)}, u32[]{:S(2)}) %collective-permute-start.7) | collective-permute-done | bytes 589856 | tf_op jit(solution)/shard_map/ppermute | solution.py:447
  638.9 1.5 collective-permute-start.8
  640.5 7.5 compare_select_fusion.5
  648.1 0.6 dynamic_slice.30
  648.8 0.7 fusion.28
  649.5 7.4 compare_select_fusion.7
  657.0 1.3 concatenate.16.tab
  658.3 49.1 %collective-permute-done.8.piv3 = f32[192,768]{1,0:T(8,128)S(1)} collective-permute-done((f32[192,768]{1,0:T(8,128)}, f32[192,768]{1,0:T(8,128)S(1)}, u32[]{:S(2)}, u32[]{:S(2)}) %collective-permute-start.8) | collective-permute-done | bytes 589856 | tf_op jit(solution)/shard_map/ppermute | solution.py:447
  707.4 1.5 collective-permute-start.10
  708.9 0.5 collective-permute-start.11
  709.5 48.0 %second_front_pivot.1 = (f32[192,768]{1,0:T(8,128)}, f32[768,768]{1,0:T(8,128)}, f32[108,128,128]{2,1,0:T(8,128)}) custom-call(s32[389]{0:T(512)} %concatenate.16.tab, f32[21,128,128]{2,1,0:T(8,128)} %get-tuple-element.31.own0, f32[36,128,128]{2,1,0:T(8,128)} %get-tuple-element.35.cross0, f32[21,128,128]{2,1,0:T(8,128)} %copy-done, ...), custom_call_target="tpu_custom_call" | custom-call | flops 16777216000 | bytes 18874368 | tf_op jit(solution)/shard_map/second_front_pivot/pallas_call | solution.py:662
  757.5 0.2 collective-permute-done.11.coup3
  757.7 0.8 copy-done.27
  758.5 0.4 copy-done.28
  758.9 18.1 %second_front_rows.1 = (f32[384,768]{1,0:T(8,128)}, f32[384,1536]{1,0:T(8,128)}) custom-call(s32[389]{0:T(512)} %concatenate.16.tab, f32[108,128,128]{2,1,0:T(8,128)} %get-tuple-element.38.g, f32[768,768]{1,0:T(8,128)} %get-tuple-element.39.inv, f32[18,128,128]{2,1,0:T(8,128)} %get-tuple-element.40.coup0, f32[18,128,128]{2,1,0:T(8,128)} %copy-done.26, ...), custom_call_target="tpu_custom_call" | custom-call | flops 4194304000 | bytes 19660800 | tf_op jit(solution)/shard_map/second_front_rows/pallas_call | solution.py:681
  (84 shorter events, 1.4 us)
Async XLA Ops:
  89.8 340.3 %collective-permute-start = (f32[42,128,128]{2,1,0:T(8,128)}, f32[42,128,128]{2,1,0:T(8,128)}, u32[]{:S(2)}, u32[]{:S(2)}) collective-permute-start(f32[42,128,128]{2,1,0:T(8,128)} %pack_first.1), channel_id=1, source_target_pairs={{0,16},{4,20},{8,24},{12,28},{16,0},{20,4},{24,8},{28,12},{1,17},{... | collective-permute-start | bytes 8257544 | tf_op jit(solution)/shard_map/ppermute | solution.py:447
  94.9 328.0 %copy-start.24 = (s32[36]{0:T(128)S(1)}, s32[36]{0:T(128)}, u32[]{:S(2)}) copy-start(s32[36]{0:T(128)} %constant.279) | copy-start | bytes 436
  94.9 328.8 %copy-start.23 = (s32[36]{0:T(128)S(1)}, s32[36]{0:T(128)}, u32[]{:S(2)}) copy-start(s32[36]{0:T(128)} %constant.280) | copy-start | bytes 436
  419.9 135.2 %collective-permute-start.1 = (f32[36,128,128]{2,1,0:T(8,128)}, f32[36,128,128]{2,1,0:T(8,128)}, u32[]{:S(2)}, u32[]{:S(2)}) collective-permute-start(f32[36,128,128]{2,1,0:T(8,128)} %get-tuple-element.25.coup), channel_id=1, source_target_pairs={{0,16},{4,20},{8,24},{12,28},{16,0},{20,4},{24,8},{28,12},{1,17},{... | collective-permute-start | bytes 7077896 | tf_op jit(solution)/shard_map/ppermute | solution.py:447
  420.0 177.1 %collective-permute-start.2 = (f32[21,128,128]{2,1,0:T(8,128)}, f32[21,128,128]{2,1,0:T(8,128)S(1)}, u32[]{:S(2)}, u32[]{:S(2)}) collective-permute-start(f32[21,128,128]{2,1,0:T(8,128)} %get-tuple-element.26.own), channel_id=1, source_target_pairs={{0,16},{4,20},{8,24},{12,28},{16,0},{20,4},{24,8},{28,12},{1,17},{... | collective-permute-start | bytes 4128776 | tf_op jit(solution)/shard_map/ppermute | solution.py:447
  555.1 18.1 %copy-start.29 = (f32[1,1,192,768]{3,2,1,0:T(8,128)S(1)}, f32[1,1,192,768]{3,2,1,0:T(8,128)}, u32[]{:S(2)}) copy-start(f32[1,1,192,768]{3,2,1,0:T(8,128)} %param.30) | copy-start | bytes 1769476
  571.4 69.0 %copy-start.1 = (pred[78]{0:T(512)(128)(4,1)S(1)}, pred[78]{0:T(512)(128)(4,1)}, u32[]{:S(2)}) copy-start(pred[78]{0:T(512)(128)(4,1)} %constant.284) | copy-start | bytes 238
  571.4 69.0 %copy-start.2 = (pred[78]{0:T(512)(128)(4,1)S(1)}, pred[78]{0:T(512)(128)(4,1)}, u32[]{:S(2)}) copy-start(pred[78]{0:T(512)(128)(4,1)} %constant.285) | copy-start | bytes 238
  571.4 69.0 %copy-start.3 = (pred[78]{0:T(512)(128)(4,1)S(1)}, pred[78]{0:T(512)(128)(4,1)}, u32[]{:S(2)}) copy-start(pred[78]{0:T(512)(128)(4,1)} %constant.286) | copy-start | bytes 238
  571.4 69.0 %copy-start.4 = (pred[78]{0:T(512)(128)(4,1)S(1)}, pred[78]{0:T(512)(128)(4,1)}, u32[]{:S(2)}) copy-start(pred[78]{0:T(512)(128)(4,1)} %constant.287) | copy-start | bytes 238
  571.4 69.0 %copy-start.5 = (pred[78]{0:T(512)(128)(4,1)S(1)}, pred[78]{0:T(512)(128)(4,1)}, u32[]{:S(2)}) copy-start(pred[78]{0:T(512)(128)(4,1)} %constant.288) | copy-start | bytes 238
  571.4 69.0 %copy-start.6 = (pred[78]{0:T(512)(128)(4,1)S(1)}, pred[78]{0:T(512)(128)(4,1)}, u32[]{:S(2)}) copy-start(pred[78]{0:T(512)(128)(4,1)} %constant.289) | copy-start | bytes 238
  571.4 69.0 %copy-start.7 = (pred[78]{0:T(512)(128)(4,1)S(1)}, pred[78]{0:T(512)(128)(4,1)}, u32[]{:S(2)}) copy-start(pred[78]{0:T(512)(128)(4,1)} %constant.290) | copy-start | bytes 238
  571.4 69.0 %copy-start.8 = (pred[78]{0:T(512)(128)(4,1)S(1)}, pred[78]{0:T(512)(128)(4,1)}, u32[]{:S(2)}) copy-start(pred[78]{0:T(512)(128)(4,1)} %constant.291) | copy-start | bytes 238
  571.5 69.0 %copy-start.9 = (pred[78]{0:T(512)(128)(4,1)S(1)}, pred[78]{0:T(512)(128)(4,1)}, u32[]{:S(2)}) copy-start(pred[78]{0:T(512)(128)(4,1)} %constant.292) | copy-start | bytes 238
  571.5 68.9 %copy-start.10 = (pred[78]{0:T(512)(128)(4,1)S(1)}, pred[78]{0:T(512)(128)(4,1)}, u32[]{:S(2)}) copy-start(pred[78]{0:T(512)(128)(4,1)} %constant.293) | copy-start | bytes 238
  571.5 68.9 %copy-start.11 = (pred[78]{0:T(512)(128)(4,1)S(1)}, pred[78]{0:T(512)(128)(4,1)}, u32[]{:S(2)}) copy-start(pred[78]{0:T(512)(128)(4,1)} %constant.294) | copy-start | bytes 238
  571.5 68.9 %copy-start.12 = (pred[78]{0:T(512)(128)(4,1)S(1)}, pred[78]{0:T(512)(128)(4,1)}, u32[]{:S(2)}) copy-start(pred[78]{0:T(512)(128)(4,1)} %constant.297) | copy-start | bytes 238
  571.5 68.9 %copy-start.13 = (pred[78]{0:T(512)(128)(4,1)S(1)}, pred[78]{0:T(512)(128)(4,1)}, u32[]{:S(2)}) copy-start(pred[78]{0:T(512)(128)(4,1)} %constant.298) | copy-start | bytes 238
  571.5 68.9 %copy-start.14 = (pred[78]{0:T(512)(128)(4,1)S(1)}, pred[78]{0:T(512)(128)(4,1)}, u32[]{:S(2)}) copy-start(pred[78]{0:T(512)(128)(4,1)} %constant.299) | copy-start | bytes 238
  571.5 68.9 %copy-start.15 = (pred[78]{0:T(512)(128)(4,1)S(1)}, pred[78]{0:T(512)(128)(4,1)}, u32[]{:S(2)}) copy-start(pred[78]{0:T(512)(128)(4,1)} %constant.300) | copy-start | bytes 238
  571.5 68.9 %copy-start.16 = (pred[78]{0:T(512)(128)(4,1)S(1)}, pred[78]{0:T(512)(128)(4,1)}, u32[]{:S(2)}) copy-start(pred[78]{0:T(512)(128)(4,1)} %constant.301) | copy-start | bytes 238
  571.6 68.9 %copy-start.17 = (pred[78]{0:T(512)(128)(4,1)S(1)}, pred[78]{0:T(512)(128)(4,1)}, u32[]{:S(2)}) copy-start(pred[78]{0:T(512)(128)(4,1)} %constant.302) | copy-start | bytes 238
  571.6 68.9 %copy-start.18 = (pred[78]{0:T(512)(128)(4,1)S(1)}, pred[78]{0:T(512)(128)(4,1)}, u32[]{:S(2)}) copy-start(pred[78]{0:T(512)(128)(4,1)} %constant.303) | copy-start | bytes 238
  571.6 68.9 %copy-start.19 = (pred[78]{0:T(512)(128)(4,1)S(1)}, pred[78]{0:T(512)(128)(4,1)}, u32[]{:S(2)}) copy-start(pred[78]{0:T(512)(128)(4,1)} %constant.304) | copy-start | bytes 238
  571.6 68.9 %copy-start.20 = (pred[78]{0:T(512)(128)(4,1)S(1)}, pred[78]{0:T(512)(128)(4,1)}, u32[]{:S(2)}) copy-start(pred[78]{0:T(512)(128)(4,1)} %constant.305) | copy-start | bytes 238
  571.6 68.9 %copy-start.21 = (pred[78]{0:T(512)(128)(4,1)S(1)}, pred[78]{0:T(512)(128)(4,1)}, u32[]{:S(2)}) copy-start(pred[78]{0:T(512)(128)(4,1)} %constant.306) | copy-start | bytes 238
  571.6 68.9 %copy-start.22 = (pred[78]{0:T(512)(128)(4,1)S(1)}, pred[78]{0:T(512)(128)(4,1)}, u32[]{:S(2)}) copy-start(pred[78]{0:T(512)(128)(4,1)} %constant.307) | copy-start | bytes 238
  571.6 76.4 %copy-start.25 = (s32[2,4]{1,0:T(2,128)S(1)}, s32[2,4]{1,0:T(2,128)}, u32[]{:S(2)}) copy-start(s32[2,4]{1,0:T(2,128)} %param.37) | copy-start | bytes 100
  571.6 137.8 %collective-permute-start.4 = (f32[36,128,128]{2,1,0:T(8,128)}, f32[36,128,128]{2,1,0:T(8,128)}, u32[]{:S(2)}, u32[]{:S(2)}) collective-permute-start(f32[36,128,128]{2,1,0:T(8,128)} %get-tuple-element.35.cross0), channel_id=1, source_target_pairs={{0,2},{1,3},{2,0},{3,1},{4,6},{5,7},{6,4},{7,5},{8,10},{9,11},{10,... | collective-permute-start | bytes 7077896 | tf_op jit(solution)/shard_map/ppermute | solution.py:447
  573.2 35.5 %collective-permute-start.6 = (f32[192,768]{1,0:T(8,128)S(1)}, f32[192,768]{1,0:T(8,128)}, u32[]{:S(2)}, u32[]{:S(2)}) collective-permute-start(f32[192,768]{1,0:T(8,128)S(1)} %bitcast.72), channel_id=1, source_target_pairs={{0,16},{4,20},{8,24},{12,28},{16,0},{20,4},{24,8},{28,12},{1,17},{... | collective-permute-start | bytes 1769480 | tf_op jit(solution)/shard_map/ppermute | solution.py:447
  573.2 65.6 %collective-permute-start.7 = (f32[192,768]{1,0:T(8,128)S(1)}, f32[192,768]{1,0:T(8,128)}, u32[]{:S(2)}, u32[]{:S(2)}) collective-permute-start(f32[192,768]{1,0:T(8,128)S(1)} %bitcast.73), channel_id=1, source_target_pairs={{0,2},{1,3},{2,0},{3,1},{4,6},{5,7},{6,4},{7,5},{8,10},{9,11},{10,... | collective-permute-start | bytes 1769480 | tf_op jit(solution)/shard_map/ppermute | solution.py:447
  598.6 110.8 %copy-start = (f32[21,128,128]{2,1,0:T(8,128)}, f32[21,128,128]{2,1,0:T(8,128)S(1)}, u32[]{:S(2)}) copy-start(f32[21,128,128]{2,1,0:T(8,128)S(1)} %add.498.oth0) | copy-start | bytes 4128772
  598.6 110.8 %collective-permute-start.5 = (f32[21,128,128]{2,1,0:T(8,128)S(1)}, f32[21,128,128]{2,1,0:T(8,128)}, u32[]{:S(2)}, u32[]{:S(2)}) collective-permute-start(f32[21,128,128]{2,1,0:T(8,128)S(1)} %add.498.oth0), channel_id=1, source_target_pairs={{0,2},{1,3},{2,0},{3,1},{4,6},{5,7},{6,4},{7,5},{8,10},{9,11},{10,... | collective-permute-start | bytes 4128776 | tf_op jit(solution)/shard_map/ppermute | solution.py:447
  600.2 109.2 %collective-permute-start.3 = (f32[21,128,128]{2,1,0:T(8,128)}, f32[21,128,128]{2,1,0:T(8,128)}, u32[]{:S(2)}, u32[]{:S(2)}) collective-permute-start(f32[21,128,128]{2,1,0:T(8,128)} %get-tuple-element.31.own0), channel_id=1, source_target_pairs={{0,2},{1,3},{2,0},{3,1},{4,6},{5,7},{6,4},{7,5},{8,10},{9,11},{10,... | collective-permute-start | bytes 4128776 | tf_op jit(solution)/shard_map/ppermute | solution.py:447
  608.7 100.2 %collective-permute-start.9 = (f32[18,128,128]{2,1,0:T(8,128)}, f32[18,128,128]{2,1,0:T(8,128)S(1)}, u32[]{:S(2)}, u32[]{:S(2)}) collective-permute-start(f32[18,128,128]{2,1,0:T(8,128)} %get-tuple-element.40.coup0), channel_id=1, source_target_pairs={{0,16},{4,20},{8,24},{12,28},{16,0},{20,4},{24,8},{28,12},{1,17},{... | collective-permute-start | bytes 3538952 | tf_op jit(solution)/shard_map/ppermute | solution.py:447
  638.9 68.5 %collective-permute-start.8 = (f32[192,768]{1,0:T(8,128)}, f32[192,768]{1,0:T(8,128)S(1)}, u32[]{:S(2)}, u32[]{:S(2)}) collective-permute-start(f32[192,768]{1,0:T(8,128)} %collective-permute-done.6.piv1), channel_id=1, source_target_pairs={{0,2},{1,3},{2,0},{3,1},{4,6},{5,7},{6,4},{7,5},{8,10},{9,11},{10,... | collective-permute-start | bytes 1769480 | tf_op jit(solution)/shard_map/ppermute | solution.py:447
  707.4 2.1 copy-start.30
  707.4 50.1 %collective-permute-start.10 = (f32[18,128,128]{2,1,0:T(8,128)}, f32[18,128,128]{2,1,0:T(8,128)S(1)}, u32[]{:S(2)}, u32[]{:S(2)}) collective-permute-start(f32[18,128,128]{2,1,0:T(8,128)} %get-tuple-element.40.coup0), channel_id=1, source_target_pairs={{0,2},{1,3},{2,0},{3,1},{4,6},{5,7},{6,4},{7,5},{8,10},{9,11},{10,... | collective-permute-start | bytes 3538952 | tf_op jit(solution)/shard_map/ppermute | solution.py:447
  708.9 48.5 %copy-start.26 = (f32[18,128,128]{2,1,0:T(8,128)}, f32[18,128,128]{2,1,0:T(8,128)S(1)}, u32[]{:S(2)}) copy-start(f32[18,128,128]{2,1,0:T(8,128)S(1)} %collective-permute-done.9.coup1) | copy-start | bytes 3538948
  708.9 48.8 %collective-permute-start.11 = (f32[18,128,128]{2,1,0:T(8,128)S(1)}, f32[18,128,128]{2,1,0:T(8,128)S(1)}, u32[]{:S(2)}, u32[]{:S(2)}) collective-permute-start(f32[18,128,128]{2,1,0:T(8,128)S(1)} %collective-permute-done.9.coup1), channel_id=1, source_target_pairs={{0,2},{1,3},{2,0},{3,1},{4,6},{5,7},{6,4},{7,5},{8,10},{9,11},{10,... | collective-permute-start | bytes 3538952 | tf_op jit(solution)/shard_map/ppermute | solution.py:447
  757.5 1.1 copy-start.27
  757.7 1.2 copy-start.28

commit v2 on v1

--- a/solution.py
+++ b/solution.py
@@ -23,11 +23,25 @@
 TRI_C = [(a, b) for a in range(CT) for b in range(a + 1)]
 TRI_U = [(a, b) for a in range(HALF_U) for b in range(a + 1)]
 TRI_P = [(a, b) for a in range(P1T // 2) for b in range(a + 1)]
+BELOW_C = [(a, b) for a, b in TRI_C if a != b]
+BELOW_U = [(a, b) for a, b in TRI_U if a != b]
+BELOW_P = [(a, b) for a, b in TRI_P if a != b]
+DIAG_FIRST = CT + P1T // 2
+N_FIRST = len(BELOW_C) + len(BELOW_P) + (DIAG_FIRST + 1) // 2
+N_OWN = len(BELOW_U) + (HALF_U + 1) // 2
+UNITS = SECOND // HALF
+OWN_UNITS = UNITS // 4
+REACH = UNITS // 2 + 1
+N_UNIT = OWN_UNITS * REACH
+N_WIDE = (N_UNIT + 1) // 2
+N_TWO = QUARTER * P2T
+N_TWO_A = N_TWO // 2
 N_OFF = (P1T // 2) ** 2
 N_PIV = P1T * P1T
 N_COUP = HALF_U * P1T
 N_TRI = len(TRI_U)
 N_CROSS = HALF_U * HALF_U
+N_CROSS_A = N_CROSS // 2
 S_COUP = N_PIV
 S_OWN = S_COUP + N_COUP
 S_FAR = S_OWN + N_TRI
@@ -53,6 +67,19 @@
         return lax.dot_general(p, q, dims, preferred_element_type=F32)
 
     return one(a[0], b[0]) + (one(a[0], b[1]) + one(a[1], b[0]))
+
+
+def times_inverse(block, parts):
+    wide = 2 * TILE
+    size = parts[0].shape[0]
+    block = split(block)
+    return jnp.concatenate(
+        [
+            dot3([p[:, : c + wide] for p in block], [q[c : c + wide, : c + wide] for q in parts], NT)
+            for c in range(0, size, wide)
+        ],
+        axis=1,
+    )
 
 
 def mul(a, b, dims):
@@ -112,12 +139,13 @@
     return both[:, :HALF], both[:, HALF:]
 
 
-def factor(a, low, inv, tiles, width):
-    d = a[0:TILE, 0:TILE]
+def factor(a, low, inv, tiles, width, start=0, stop=None):
+    stop = tiles if stop is None else stop
+    d = a[start * TILE : (start + 1) * TILE, start * TILE : (start + 1) * TILE]
     zero = jnp.zeros((HALF, HALF), F32)
     ri = lax.broadcasted_iota(jnp.int32, (HALF, HALF), 0)
     ci = lax.broadcasted_iota(jnp.int32, (HALF, HALF), 1)
-    for k in range(tiles):
+    for k in range(start, stop):
         k0, k1, k2 = k * TILE, (k + 1) * TILE, (k + 2) * TILE
         u1, w1 = factor_half(d[:HALF, :HALF], width)
         l21 = mul(d[HALF:, :HALF], w1, NT)
@@ -151,6 +179,8 @@
             rest = jnp.zeros((TILE, (tiles - k - 1) * TILE), F32)
             low[k0:k1, k1:] = rest
             inv[k0:k1, k1:] = rest
+    if stop < tiles:
+        a[k1:k2, k1:k2] = d
 
 
 def padded(a, tile_of, live, tiles):
@@ -180,20 +210,73 @@
     ]
 
 
-def pack_first(tab, block, pivot, out, sems):
+def square_index():
+    return (
+        lax.broadcasted_iota(jnp.int32, (TILE, TILE), 0),
+        lax.broadcasted_iota(jnp.int32, (TILE, TILE), 1),
+    )
+
+
+def put_pairs(tiles_in, out, first):
+    r, c = square_index()
+    diagonals = []
+    for n in range(0, len(tiles_in), 2):
+        mixed = tiles_in[n]
+        if n + 1 < len(tiles_in):
+            mixed = jnp.where(r >= c, mixed, tiles_in[n + 1])
+            diagonals.append(jnp.sum(jnp.where(r == c, tiles_in[n + 1], 0.0), axis=0, keepdims=True))
+        out[pl.ds((first + n // 2) * TILE, TILE), :] = mixed
+    diagonals += [jnp.zeros((1, TILE), F32)] * (ROWS - len(diagonals))
+    out[pl.ds((first + (len(tiles_in) + 1) // 2) * TILE, ROWS), :] = jnp.concatenate(diagonals, axis=0)
+
+
+def get_pairs(ref, first, count):
+    r, c = square_index()
+    base = (first + (count + 1) // 2) * TILE
+    out = []
+    for n in range(0, count, 2):
+        mixed = ref[(first + n // 2) * TILE : (first + n // 2 + 1) * TILE, :]
+        if n + 1 == count:
+            out.append(mixed)
+            continue
+        other = mixed.T
+        out.append(jnp.where(r >= c, mixed, other))
+        diagonal = ref[base + n // 2 : base + n // 2 + 1, :]
+        out.append(jnp.where(r == c, diagonal, jnp.where(r < c, mixed, other)))
+    return out
+
+
+def message_tile(ref, n):
+    return ref[pl.ds(pl.multiple_of(n * TILE, TILE), TILE), :]
+
+
+def pack_first(tab, block, pivot, out, square, sems):
     side = tab[CT]
     pairs = []
-    for n, (a, b) in enumerate(TRI_C):
-        pairs.append((tile_at(block, tab[a], tab[b]), out.at[n]))
-    for n, (a, b) in enumerate(TRI_P):
-        pairs.append((tile_at(pivot, a, side * (P1T // 2) + b), out.at[len(TRI_C) + n]))
+    for n, (a, b) in enumerate(BELOW_C):
+        pairs.append((tile_at(block, tab[a], tab[b]), out.at[pl.ds(n * TILE, TILE)]))
+    first = len(BELOW_C)
+    for n, (a, b) in enumerate(BELOW_P):
+        pairs.append(
+            (tile_at(pivot, a, side * (P1T // 2) + b), out.at[pl.ds((first + n) * TILE, TILE)])
+        )
+    for a in range(CT):
+        pairs.append((tile_at(block, tab[a], tab[a]), square.at[a]))
+    for a in range(P1T // 2):
+        pairs.append((tile_at(pivot, a, side * (P1T // 2) + a), square.at[CT + a]))
     copy_all(pairs, sems)
-
-
-def pack_rest(tab, block, pivot, rows, second, coup, own, kept, cross, off, coup_two, sems):
+    put_pairs([square[n] for n in range(DIAG_FIRST)], out, first + len(BELOW_P))
+
+
+def pack_rest(
+    tab, block, pivot, rows, pivot_second, second,
+    coup, own, kept, cross, off, own_sent, coup_two, two_sent_a, two_sent_b, units, units_sent,
+    strips, sems,
+):
     side = tab[CT]
     order = CT + 1
     local = order + CT
+    quarter = tab[local + U1T]
     pairs = []
     for r in range(HALF_U):
         row = tab[local + r] - side * HALF_U
@@ -219,8 +302,48 @@
         pairs.append((tile_at(pivot, i, side * (P1T // 2) + k), off.at[N_OFF + n]))
     for r in range(QUARTER):
         for c in range(P2T):
-            pairs.append((tile_at(second, r, c), coup_two.at[r * P2T + c]))
+            n = r * P2T + c
+            sent = two_sent_a.at[n] if n < N_TWO_A else two_sent_b.at[n - N_TWO_A]
+            pairs.append((tile_at(second, r, c), coup_two.at[n]))
+            pairs.append((tile_at(second, r, c), sent))
+    far = []
+    for i in range(OWN_UNITS):
+        for d in range(REACH):
+            col = (quarter * OWN_UNITS + i - d + UNITS) % UNITS
+            far.append(col % 2)
+            source = pivot_second.at[
+                pl.ds(i * HALF, HALF), pl.ds(pl.multiple_of(col // 2 * TILE, TILE), TILE)
+            ]
+            pairs.append((source, strips.at[i * REACH + d]))
     copy_all(pairs, sems)
+    lane = lax.broadcasted_iota(jnp.int32, (HALF, TILE), 1)
+
+    def placed(n, half):
+        strip = strips[n]
+        return jnp.where(far[n] == half, strip, pltpu.roll(strip, HALF, 1))
+
+    for n in range(N_WIDE):
+        strip = placed(2 * n, 0)
+        if 2 * n + 1 < N_UNIT:
+            strip = jnp.where(lane < HALF, strip, placed(2 * n + 1, 1))
+        units[n * HALF : (n + 1) * HALF, :] = strip
+        units_sent[n * HALF : (n + 1) * HALF, :] = strip
+    put_own([own[n] for n in range(N_TRI)], own_sent)
+
+
+def after(array, *others):
+    def kernel(*refs):
+        pass
+
+    return pl.pallas_call(
+        kernel,
+        out_shape=jax.ShapeDtypeStruct(array.shape, array.dtype),
+        in_specs=[HBM] * (1 + len(others)),
+        out_specs=HBM,
+        input_output_aliases={0: 0},
+        name="after",
+        cost_estimate=CHEAP,
+    )(array, *others)
 
 
 T_SIDE = 0
@@ -228,7 +351,7 @@
 T_LOCAL = 2
 T_FILL = T_LOCAL + U1T
 T_SLOT = T_FILL + U1T * P1T
-T_SLOT_FAR = T_SLOT + len(TRI_C)
+T_SLOT_FAR = T_SLOT + CT * CT
 
 
 def panel_rows(tile_of, count, live, inv, put):
@@ -243,7 +366,7 @@
         )
         lane = lax.broadcasted_iota(jnp.int32, block.shape, 1)
         block = jnp.where(lane < live * TILE, block, 0.0)
-        put(r, dot3(split(block), parts, NT))
+        put(r, times_inverse(block, parts))
 
 
 def first_kernel(
@@ -254,10 +377,15 @@
     side = tab[T_SIDE]
     live = tab[T_LIVE]
     half = P1T // 2
+    square = get_pairs(theirs, len(BELOW_C) + len(BELOW_P), DIAG_FIRST)
     front[0:N_PIV] = jnp.zeros((N_PIV, TILE, TILE), F32)
     for n, (i, k) in enumerate(TRI_P):
         front[(side * half + i) * P1T + side * half + k] = off[N_OFF + n]
-        front[((1 - side) * half + i) * P1T + (1 - side) * half + k] = theirs[len(TRI_C) + n]
+        if i == k:
+            tile = square[CT + i]
+        else:
+            tile = message_tile(theirs, len(BELOW_C) + BELOW_P.index((i, k)))
+        front[((1 - side) * half + i) * P1T + (1 - side) * half + k] = tile
     for i in range(half):
         for k in range(half):
 
@@ -283,15 +411,23 @@
         return carry
 
     lax.fori_loop(0, N_TRI, copy, 0)
-
-    def extend(n, carry):
-        here = tab[T_SLOT + n]
-        front[here] = front[here] + mine[n]
-        there = tab[T_SLOT_FAR + n]
-        front[there] = front[there] + theirs[n]
-        return carry
-
-    lax.fori_loop(0, len(TRI_C), extend, 0)
+    for i in range(CT):
+
+        def extend(k, carry, i=i):
+            here = tab[T_SLOT + i * CT + k]
+            front[here] = front[here] + mine[tri(i, 0) + k]
+            return carry
+
+        lax.fori_loop(0, i + 1, extend, 0)
+
+        def extend_far(k, carry, i=i):
+            there = tab[T_SLOT_FAR + i * CT + k]
+            front[there] = front[there] + message_tile(theirs, i * (i - 1) // 2 + k)
+            return carry
+
+        lax.fori_loop(0, i, extend_far, 0)
+        there = tab[T_SLOT_FAR + i * CT + i]
+        front[there] = front[there] + square[i]
     leave = pltpu.make_async_copy(front.at[pl.ds(S_FAR, N_FRONT - S_FAR)], far_out, sem)
     leave.start()
     padded(a, lambda i, j: front[i * P1T + j], live, P1T)
@@ -311,12 +447,11 @@
         left = split(panel_out[i * TILE : (i + 1) * TILE, :])
         product = dot3(left, split(panel_out[0 : (i + 1) * TILE, :]), NT)
         for k in range(i + 1):
-            n = i * (i + 1) // 2 + k
-            own_out[n] = front[S_OWN + n] - product[:, k * TILE : (k + 1) * TILE]
+            own_out[tri(i, k)] = front[S_OWN + tri(i, k)] - product[:, k * TILE : (k + 1) * TILE]
     leave.wait()
 
 
-def second_kernel(tab, far, coup, inv, panel, cross_out, oth_out, panel_far):
+def second_kernel(tab, far, coup, inv, panel, cross_a, cross_b, oth_out, panel_far):
     live = tab[T_LIVE]
 
     def tile_of(r, c):
@@ -333,7 +468,8 @@
         for q in range(2):
             for k in range(HALF_U):
                 n = (i + q) * HALF_U + k
-                cross_out[n] = (
+                out, first = (cross_a, 0) if n < N_CROSS_A else (cross_b, N_CROSS_A)
+                out[n - first] = (
                     far[N_COUP + n]
                     - product[q * TILE : (q + 1) * TILE, k * TILE : (k + 1) * TILE]
                 )
@@ -341,105 +477,221 @@
         left = split(panel_far[i * TILE : (i + 1) * TILE, :])
         product = dot3(left, split(panel_far[0 : (i + 1) * TILE, :]), NT)
         for k in range(i + 1):
-            n = i * (i + 1) // 2 + k
-            oth_out[n] = far[N_COUP + N_CROSS + n] - product[:, k * TILE : (k + 1) * TILE]
+            oth_out[tri(i, k)] = (
+                far[N_COUP + N_CROSS + tri(i, k)] - product[:, k * TILE : (k + 1) * TILE]
+            )
+
+
+def add_kernel(part, got, out, sent):
+    square = get_pairs(got, len(BELOW_U), HALF_U)
+    for n, (i, k) in enumerate(BELOW_U):
+        out[tri(i, k)] = part[tri(i, k)] + message_tile(got, n)
+    for i in range(HALF_U):
+        out[tri(i, i)] = part[tri(i, i)] + square[i]
+    put_own([out[n] for n in range(N_TRI)], sent)
+
+
+def put_own(block, out):
+    for n, (a, b) in enumerate(BELOW_U):
+        out[n * TILE : (n + 1) * TILE, :] = block[tri(a, b)]
+    put_pairs([block[tri(a, a)] for a in range(HALF_U)], out, len(BELOW_U))
+
+
+def get_own(ref, out):
+    for n, (i, k) in enumerate(BELOW_U):
+        out[tri(i, k)] = message_tile(ref, n)
+    for i, tile in enumerate(get_pairs(ref, len(BELOW_U), HALF_U)):
+        out[tri(i, i)] = tile
 
 
 Q_LIVE = 0
 Q_MINE = 1
 Q_FILL = 5
 Q_DIRECT = Q_FILL + U2T * P2T
-N_S1 = 2 * N_TRI + N_CROSS
-Q_TURNED = Q_DIRECT + 2 * N_S1
-
-
-def third_kernel(
-    tab, own0, cross0, oth0, own1, cross1, oth1, piv0, piv1, piv2, piv3, second,
-    lower_out, inv_out, g_out,
-    g, a, low, sem,
-):
-    units = SECOND // 4 // HALF
-    for s, piv in enumerate((piv0, piv1, piv2, piv3)):
-        for i in range(units):
-            unit = tab[Q_MINE + s] * units + i
-            row = unit // 2
-            start = pl.multiple_of((unit % 2) * HALF, HALF)
-            for c in range(P2T):
-                g[row * P2T + c, pl.ds(start, HALF), :] = piv[
-                    i * HALF : (i + 1) * HALF, c * TILE : (c + 1) * TILE
-                ]
-
+Q_TURNED = Q_DIRECT + 2 * U1T * U1T
+
+
+def extend_cross(tab, refs, g, front, low, high):
+    for q, ref in enumerate(refs):
+        extend_two(tab, ref, g, front, q * HALF_U // 2, HALF_U, False, low, high, HALF_U // 2)
+
+
+def extend_two(tab, ref, g, front, rows, cols, triangle, low, high, count=HALF_U):
+    for i in range(count):
+
+        def one(k, carry, i=i):
+            at = front * U1T * U1T + (rows + i) * U1T + cols + k
+            n = (tri(i, 0) if triangle else i * HALF_U) + k
+            direct = tab[Q_DIRECT + at]
+            turned = tab[Q_TURNED + at]
+
+            @pl.when((direct >= low) & (direct < high))
+            def _():
+                g[direct - low] = g[direct - low] + ref[n]
+
+            @pl.when((turned >= low) & (turned < high))
+            def _():
+                g[turned - low] = g[turned - low] + ref[n].T
+
+            return carry
+
+        lax.fori_loop(0, i + 1 if triangle else HALF_U, one, 0)
+
+
+def add_units(tab, g, units, s):
+    lane = lax.broadcasted_iota(jnp.int32, (HALF, TILE), 1)
+    for i in range(OWN_UNITS):
+        row = tab[Q_MINE + s] * OWN_UNITS + i
+        for d in range(REACH):
+            n = i * REACH + d
+            col = (row - d + UNITS) % UNITS
+            strip = units[n // 2 * HALF : (n // 2 + 1) * HALF, :]
+            here = n % 2
+
+            def add(r, c, block):
+                slot = r // 2 * P2T + c // 2
+                start = pl.multiple_of(r % 2 * HALF, HALF)
+                old = g[slot, pl.ds(start, HALF), :]
+                g[slot, pl.ds(start, HALF), :] = old + jnp.where(lane // HALF == c % 2, block, 0.0)
+
+            @pl.when((col <= row) & ((d < REACH - 1) | (row >= UNITS // 2)))
+            def _():
+                add(row, col, jnp.where(col % 2 == here, strip, pltpu.roll(strip, HALF, 1)))
+
+            if d < REACH - 1 and d > 0:
+
+                @pl.when(col > row)
+                def _():
+                    turned = strip.T[here * HALF : (here + 1) * HALF, :]
+                    add(col, row, jnp.concatenate([turned, turned], axis=1))
+
+
+def third_kernel(tab, own0, cross0_a, cross0_b, own1, units0, units2, second, g):
     def clear(n, carry):
-        g[G_COUP + n] = jnp.zeros((TILE, TILE), F32)
+        g[n] = jnp.zeros((TILE, TILE), F32)
         return carry
 
-    lax.fori_loop(0, U2T * P2T, clear, 0)
+    lax.fori_loop(0, G_TRAIL, clear, 0)
     for r in range(QUARTER):
         for c in range(U2T):
             g[G_TRAIL + r * U2T + c] = second[
                 r * TILE : (r + 1) * TILE, SECOND + c * TILE : SECOND + (c + 1) * TILE
             ]
-    first = 0
-    for ref in (own0, cross0, oth0, own1, cross1, oth1):
-
-        def extend(n, carry, ref=ref, first=first):
-            direct = tab[Q_DIRECT + first + n]
-            turned = tab[Q_TURNED + first + n]
-            g[direct] = g[direct] + ref[n]
-
-            @pl.when(turned != G_NONE)
-            def _():
-                g[turned] = g[turned] + ref[n].T
-
-            return carry
-
-        lax.fori_loop(0, ref.shape[0], extend, 0)
-        first += ref.shape[0]
-    leave = pltpu.make_async_copy(g.at[pl.ds(G_COUP, G_NONE - G_COUP)], g_out, sem)
-    leave.start()
+    add_units(tab, g, units0, 0)
+    add_units(tab, g, units2, 2)
+    extend_two(tab, own0, g, 0, 0, 0, True, 0, G_NONE)
+    extend_cross(tab, (cross0_a, cross0_b), g, 0, 0, G_NONE)
+    extend_two(tab, own1, g, 1, 0, 0, True, 0, G_NONE)
+
+
+def more_kernel(tab, part, cross1_a, cross1_b, oth0, units1, g, sem):
+    enter = pltpu.make_async_copy(part, g, sem)
+    enter.start()
+    enter.wait()
+    add_units(tab, g, units1, 1)
+    extend_cross(tab, (cross1_a, cross1_b), g, 1, 0, G_NONE)
+    extend_two(tab, oth0, g, 0, HALF_U, HALF_U, True, 0, G_NONE)
+
+
+def pivot_kernel(tab, part, oth1, units3, a, low, inv_out, g, other, sem):
+    enter = pltpu.make_async_copy(part.at[pl.ds(0, G_COUP)], g, sem)
+    enter.start()
+    get_own(oth1, other)
+    enter.wait()
+    add_units(tab, g, units3, 3)
+    extend_two(tab, other, g, 1, HALF_U, HALF_U, True, 0, G_COUP)
     padded(a, lambda i, j: g[i * P2T + j], tab[Q_LIVE], P2T)
-    factor(a, low, inv_out, P2T, 8)
+    factor(a, low, inv_out, P2T, 8, 0, P2T // 2)
+
+
+def pivot_rest_kernel(tab, a_in, low_in, inv_in, lower_out, inv_out, a, low):
+    done = P2T // 2 * TILE
+    a[done:, done:] = a_in[done:, done:]
+    low[:, :done] = low_in[:, :done]
+    low[:done, done:] = jnp.zeros((done, SECOND - done), F32)
+    inv_out[:done, :] = inv_in[:done, :]
+    factor(a, low, inv_out, P2T, 8, P2T // 2)
     start = tab[Q_MINE] * (SECOND // 4)
     lower_out[...] = low[pl.ds(pl.multiple_of(start, HALF), SECOND // 4), :]
-    leave.wait()
-
-
-def last_kernel(tab, g, inv, coup0, coup1, coup2, coup3, panel_out, schur_out, panels):
-    live = tab[Q_LIVE]
+
+
+def quarter_rows_of(tab, g, quarter):
+    return jnp.concatenate(
+        [
+            jnp.concatenate([g[(quarter * QUARTER + r) * P2T + c] for c in range(P2T)], axis=1)
+            for r in range(QUARTER)
+        ],
+        axis=0,
+    )
+
+
+def halves(first, second):
+    return lambda n: first[n] if n < N_TWO_A else second[n - N_TWO_A]
+
+
+def quarter_panel(tab, block, coup, parts, quarter):
+    rows = []
+    for r in range(QUARTER):
+        fill = Q_FILL + (quarter * QUARTER + r) * P2T
+        rows.append(
+            jnp.concatenate(
+                [coup(r * P2T + c) * tab[fill + c].astype(F32) for c in range(P2T)], axis=1
+            )
+        )
+    block = block + jnp.concatenate(rows, axis=0)
+    lane = lax.broadcasted_iota(jnp.int32, block.shape, 1)
+    block = jnp.where(lane < tab[Q_LIVE] * TILE, block, 0.0)
+    return times_inverse(block, parts)
+
+
+WIDE = QUARTER * TILE
+
+
+def rows_kernel(
+    tab, part, oth1, inv, coup0, coup1_a, coup1_b, coup2,
+    panel_out, schur_out, rest_out,
+    g, other, panels, sem,
+):
+    enter = pltpu.make_async_copy(part.at[pl.ds(G_COUP, G_NONE - G_COUP)], g, sem)
+    enter.start()
+    get_own(oth1, other)
+    enter.wait()
+    extend_two(tab, other, g, 1, HALF_U, HALF_U, True, G_COUP, G_NONE)
     parts = split(inv[...])
-    for s, coup in enumerate((coup0, coup1, coup2, coup3)):
+    rest_out[...] = quarter_rows_of(tab, g, tab[Q_MINE + 3])
+    whole = [lambda n, ref=ref: ref[n] for ref in (coup0, coup2)]
+    for s, coup in enumerate((whole[0], halves(coup1_a, coup1_b), whole[1])):
         quarter = tab[Q_MINE + s]
-        rows = []
-        for r in range(QUARTER):
-            row = quarter * QUARTER + r
-            rows.append(
-                jnp.concatenate(
-                    [
-                        g[row * P2T + c]
-                        + coup[r * P2T + c] * tab[Q_FILL + row * P2T + c].astype(F32)
-                        for c in range(P2T)
-                    ],
-                    axis=1,
-                )
-            )
-        block = jnp.concatenate(rows, axis=0)
-        lane = lax.broadcasted_iota(jnp.int32, block.shape, 1)
-        block = jnp.where(lane < live * TILE, block, 0.0)
-        panel = dot3(split(block), parts, NT)
-        panels[quarter] = panel
+        panel = quarter_panel(tab, quarter_rows_of(tab, g, quarter), coup, parts, quarter)
+        panels[s] = panel
         if s == 0:
             panel_out[...] = panel
     left = split(panel_out[...])
-    wide = QUARTER * TILE
-    for q in range(4):
-        product = dot3(left, split(panels[q]), NT)
+    for s in range(4):
+        quarter = tab[Q_MINE + s]
+        if s < 3:
+            product = dot3(left, split(panels[s]), NT)
         for r in range(QUARTER):
             for c in range(QUARTER):
-                col = q * QUARTER + c
-                schur_out[r * TILE : (r + 1) * TILE, col * TILE : (col + 1) * TILE] = (
-                    g[G_TRAIL - G_COUP + r * U2T + col]
-                    - product[r * TILE : (r + 1) * TILE, c * TILE : (c + 1) * TILE]
-                )
+                tile = g[G_TRAIL - G_COUP + r * U2T + quarter * QUARTER + c]
+                if s < 3:
+                    tile = tile - product[r * TILE : (r + 1) * TILE, c * TILE : (c + 1) * TILE]
+                col = pl.multiple_of((quarter * QUARTER + c) * TILE, TILE)
+                schur_out[r * TILE : (r + 1) * TILE, pl.ds(col, TILE)] = tile
+
+
+def last_kernel(tab, schur, rest, panel, inv, coup_a, coup_b, out, block, sem):
+    quarter = tab[Q_MINE + 3]
+    col = pl.ds(pl.multiple_of(quarter * WIDE, TILE), WIDE)
+    enter = pltpu.make_async_copy(schur.at[:, col], block, sem)
+    enter.start()
+    other = quarter_panel(tab, rest[...], halves(coup_a, coup_b), split(inv[...]), quarter)
+    product = dot3(split(panel[...]), split(other), NT)
+    enter.wait()
+    block[...] = block[...] - product
+    leave = pltpu.make_async_copy(block, out.at[:, col], sem)
+    leave.start()
+    leave.wait()
 
 
 def swap(array, axis):
@@ -458,11 +710,28 @@
 SMEM = pl.BlockSpec(memory_space=pltpu.SMEM)
 VMEM = pl.BlockSpec(memory_space=pltpu.VMEM)
 HBM = pl.BlockSpec(memory_space=pl.ANY)
-LIMIT = 56 << 20
-
-
-def cost(flops, count):
-    return pl.CostEstimate(flops=flops, bytes_accessed=count * TILE * TILE * 4, transcendentals=0)
+LIMIT = 60 << 20
+CHEAP = pl.CostEstimate(flops=1, bytes_accessed=1, transcendentals=0)
+
+
+def call(kernel, name, out_shape, in_specs, out_specs, scratch=(), waits=(), limit=LIMIT, **options):
+    count = len(in_specs)
+
+    def body(*refs):
+        kernel(*refs[:count], *refs[count + len(waits) :])
+
+    run = pl.pallas_call(
+        body,
+        out_shape=out_shape,
+        in_specs=in_specs + [HBM] * len(waits),
+        out_specs=out_specs,
+        scratch_shapes=list(scratch),
+        name=name,
+        compiler_params=pltpu.CompilerParams(vmem_limit_bytes=limit),
+        cost_estimate=CHEAP,
+        **options,
+    )
+    return lambda *args: run(*args, *waits)
 
 
 def tri(i, k):
@@ -495,8 +764,8 @@
 
 
 def slots(keys):
-    row = keys[np.array([a for a, b in TRI_C])]
-    col = keys[np.array([b for a, b in TRI_C])]
+    row = keys[:, None]
+    col = keys[None, :]
     own = P1T + HALF_U
     pivot = row * P1T + col
     coup = jnp.where(row >= own, S_COUP + (row - own) * P1T, S_FAR + (row - P1T) * P1T) + col
@@ -504,19 +773,12 @@
     cross = S_CROSS + (row - own) * HALF_U + col - P1T
     other = S_OTH + tri(row - P1T, col - P1T)
     rest = jnp.where(row < own, other, jnp.where(col < own, cross, near))
-    return jnp.where(row < P1T, pivot, jnp.where(col < P1T, coup, rest))
-
-
-PAIRS = (
-    TRI_U
-    + [(i, HALF_U + k) for i in range(HALF_U) for k in range(HALF_U)]
-    + [(HALF_U + i, HALF_U + k) for i, k in TRI_U]
-)
+    return jnp.where(row < P1T, pivot, jnp.where(col < P1T, coup, rest)).reshape(-1)
 
 
 def targets(goal, quarter):
-    row = goal[np.array([a for a, b in PAIRS])]
-    col = goal[np.array([b for a, b in PAIRS])]
+    row = goal[:, None]
+    col = goal[None, :]
 
     def index(r, c):
         mine = (r - P2T) // QUARTER == quarter
@@ -526,7 +788,8 @@
         return jnp.where(r < P2T, jnp.where((c < P2T) & (r >= c), r * P2T + c, G_NONE), rest)
 
     direct = index(row, col)
-    return direct, jnp.where(row == col, G_NONE, index(col, row))
+    turned = jnp.where(row == col, G_NONE, index(col, row))
+    return direct.reshape(-1), turned.reshape(-1)
 
 
 def body(
@@ -554,49 +817,49 @@
     front_hi = index_hi % half_hi
     far_lo = (index_lo + half_lo) % size_lo
     far_hi = (index_hi + half_hi) % size_hi
+    quarter = 2 * side_hi + side_lo
     block, pivot, rows = contribution[0, 0], pivot_one[0, 0], rows_one[0, 0]
     pivot_second, rows_second = pivot_two[0, 0], rows_two[0, 0]
-    params = pltpu.CompilerParams(vmem_limit_bytes=LIMIT)
 
     second_map = map_two[index_hi, front_lo]
     place, hit = local_order(second_map, side_lo)
     key = place_of(map_one[index_hi, index_lo], place)
     order_sent, _ = sort_by(key)
     tab_first = jnp.concatenate([order_sent, side_lo[None]]).astype(jnp.int32)
-    n_first = len(TRI_C) + len(TRI_P)
-    sent = pl.pallas_call(
+    sent = call(
         pack_first,
-        out_shape=tiles(n_first),
-        in_specs=[SMEM, HBM, HBM],
-        out_specs=HBM,
-        scratch_shapes=[pltpu.SemaphoreType.DMA((n_first,))],
-        name="pack_first",
-        compiler_params=params,
-        cost_estimate=cost(0, 2 * n_first),
+        "pack_first",
+        dense(N_FIRST * TILE + ROWS, TILE),
+        [SMEM, HBM, HBM],
+        VMEM,
+        [
+            pltpu.VMEM((DIAG_FIRST, TILE, TILE), F32),
+            pltpu.SemaphoreType.DMA((len(TRI_C) + len(TRI_P),)),
+        ],
     )(tab_first, block, pivot)
     got_first = swap(sent, "lo")
 
     unit = jnp.arange(U1T, dtype=jnp.int32)
     local = jnp.sum(hit * unit[None, :], axis=1)
     order_kept, keys = sort_by(turned_key(key))
-    tab_rest = jnp.concatenate([tab_first, order_kept, local]).astype(jnp.int32)
-    shapes = [tiles(N_COUP), tiles(N_TRI), tiles(len(TRI_C)), tiles(N_CROSS), tiles(N_OFF + len(TRI_P)), tiles(QUARTER * P2T)]
-    n_rest = sum(s.shape[0] for s in shapes)
-    coup, own, kept, cross, off, coup_two = pl.pallas_call(
+    tab_rest = jnp.concatenate([tab_first, order_kept, local, quarter[None]]).astype(jnp.int32)
+    shapes = [
+        tiles(N_COUP), tiles(N_TRI), tiles(len(TRI_C)), tiles(N_CROSS), tiles(N_OFF + len(TRI_P)),
+        dense(N_OWN * TILE + ROWS, TILE), tiles(N_TWO), tiles(N_TWO_A), tiles(N_TWO - N_TWO_A),
+        dense(N_WIDE * HALF, TILE), dense(N_WIDE * HALF, TILE),
+    ]
+    n_rest = N_COUP + N_TRI + len(TRI_C) + N_CROSS + N_OFF + len(TRI_P) + 2 * N_TWO + N_UNIT
+    coup, own, kept, cross, off, own_sent, two, two_a, two_b, units, units_sent = call(
         pack_rest,
-        out_shape=shapes,
-        in_specs=[SMEM, HBM, HBM, HBM, HBM],
-        out_specs=[HBM] * len(shapes),
-        scratch_shapes=[pltpu.SemaphoreType.DMA((n_rest,))],
-        name="pack_rest",
-        compiler_params=params,
-        cost_estimate=cost(0, 2 * n_rest),
-    )(tab_rest, block, pivot, rows, rows_second)
-    got_coup = swap(coup, "lo")
-    got_own = swap(own, "lo")
-    got_pivot = swap(pivot_second, "lo")
-    got_two = swap(coup_two, "lo")
-
+        "pack_rest",
+        shapes,
+        [SMEM] + [HBM] * 5,
+        [VMEM] * len(shapes),
+        [pltpu.VMEM((N_UNIT, HALF, TILE), F32), pltpu.SemaphoreType.DMA((n_rest,))],
+        waits=(sent,),
+    )(tab_rest, block, pivot, rows, pivot_second, rows_second)
+    two_hi = swap(two, "hi")
+    units_hi = swap(units, "hi")
     far_key = place_of(map_one[index_hi, far_lo], place)
     _, far_keys = sort_by(turned_key(far_key))
     live_first = live_one[index_hi, front_lo]
@@ -604,51 +867,10 @@
     tab_one = jnp.concatenate(
         [side_lo[None], live_first[None], local, fill_first.reshape(-1), slots(keys), slots(far_keys)]
     ).astype(jnp.int32)
-    mega = 2 * TILE**3
-    half_rows = HALF_U * TILE
-    lower_one, inv_one, panel_own, panel_one, s_own, far_part = pl.pallas_call(
-        first_kernel,
-        out_shape=[
-            dense(PIVOT // 2, PIVOT), dense(PIVOT, PIVOT), dense(half_rows, PIVOT),
-            dense(half_rows, PIVOT), tiles(N_TRI), tiles(N_FRONT - S_FAR),
-        ],
-        in_specs=[SMEM] + [VMEM] * 6,
-        out_specs=[VMEM] * 5 + [HBM],
-        scratch_shapes=[
-            pltpu.VMEM((N_FRONT, TILE, TILE), F32),
-            pltpu.VMEM((PIVOT, PIVOT), F32),
-            pltpu.VMEM((PIVOT, PIVOT), F32),
-            pltpu.SemaphoreType.DMA,
-        ],
-        name="first_front_own",
-        compiler_params=params,
-        cost_estimate=cost(4000 * mega, 2 * N_FRONT),
-    )(tab_one, kept, got_first, coup, own, cross, off)
-    s_own_far = swap(s_own, "hi")
-    pivot_hi, got_pivot_hi = swap(pivot_second, "hi"), swap(got_pivot, "hi")
-    two_hi = swap(coup_two, "hi")
-
-    s_cross, s_part = pl.pallas_call(
-        second_kernel,
-        out_shape=[tiles(N_CROSS), tiles(N_TRI)],
-        in_specs=[SMEM] + [VMEM] * 4,
-        out_specs=[VMEM] * 2,
-        scratch_shapes=[pltpu.VMEM((half_rows, PIVOT), F32)],
-        name="first_front_other",
-        compiler_params=params,
-        cost_estimate=cost(1500 * mega, 300),
-    )(tab_one, far_part, got_coup, inv_one, panel_own)
-    s_cross_far = swap(s_cross, "hi")
-    s_oth = s_part + got_own
-    s_oth_far = swap(s_oth, "hi")
-    two_both = swap(got_two, "hi")
-
-    quarter = 2 * side_hi + side_lo
-    _, hit_far = local_order(map_two[far_hi, front_lo], side_lo)
-    goal = jnp.sum(hit * second_map[None, :], axis=1)
-    goal_far = jnp.sum(hit_far * map_two[far_hi, front_lo][None, :], axis=1)
-    direct, turned = targets(goal, quarter)
-    direct_far, turned_far = targets(goal_far, quarter)
+    map_far = map_two[far_hi, front_lo]
+    _, hit_far = local_order(map_far, side_lo)
+    direct, turned = targets(jnp.sum(hit * second_map[None, :], axis=1), quarter)
+    direct_far, turned_far = targets(jnp.sum(hit_far * map_far[None, :], axis=1), quarter)
     fill_second = fill_two[front_hi, front_lo].reshape(-1)
     quarters = jnp.stack(
         [quarter, 2 * side_hi + 1 - side_lo, 2 * (1 - side_hi) + side_lo, 2 * (1 - side_hi) + 1 - side_lo]
@@ -659,35 +881,111 @@
             direct, direct_far, turned, turned_far,
         ]
     ).astype(jnp.int32)
-    lower_two, inv_two, gathered = pl.pallas_call(
-        third_kernel,
-        out_shape=[dense(SECOND // 4, SECOND), dense(SECOND, SECOND), tiles(G_NONE - G_COUP)],
-        in_specs=[SMEM] + [VMEM] * 11,
-        out_specs=[VMEM] * 2 + [HBM],
-        scratch_shapes=[
-            pltpu.VMEM((G_NONE + 1, TILE, TILE), F32),
-            pltpu.VMEM((SECOND, SECOND), F32),
-            pltpu.VMEM((SECOND, SECOND), F32),
+    coup = after(coup, got_first, two_hi, units_hi, tab_one, tab_two)
+    got_coup = swap(coup, "lo")
+
+    half_rows = HALF_U * TILE
+    lower_one, inv_one, panel_own, panel_one, s_own, far_part = call(
+        first_kernel,
+        "first_front_own",
+        [
+            dense(PIVOT // 2, PIVOT), dense(PIVOT, PIVOT), dense(half_rows, PIVOT),
+            dense(half_rows, PIVOT), tiles(N_TRI), tiles(N_FRONT - S_FAR),
+        ],
+        [SMEM] + [VMEM] * 6,
+        [VMEM] * 5 + [HBM],
+        [
+            pltpu.VMEM((N_FRONT, TILE, TILE), F32),
+            pltpu.VMEM((PIVOT, PIVOT), F32),
+            pltpu.VMEM((PIVOT, PIVOT), F32),
             pltpu.SemaphoreType.DMA,
         ],
-        name="second_front_pivot",
-        compiler_params=params,
-        cost_estimate=cost(4000 * mega, 2 * G_NONE),
-    )(
-        tab_two, s_own, s_cross, s_oth, s_own_far, s_cross_far, s_oth_far,
-        pivot_second, got_pivot, pivot_hi, got_pivot_hi, rows_second,
+    )(tab_one, kept, got_first, coup, own, cross, off)
+    s_own_far = swap(s_own, "hi")
+    own_sent = after(own_sent, got_coup, panel_own)
+    got_own = swap(own_sent, "lo")
+
+    cross_a, cross_b, s_part = call(
+        second_kernel,
+        "first_front_other",
+        [tiles(N_CROSS_A), tiles(N_CROSS - N_CROSS_A), tiles(N_TRI)],
+        [SMEM] + [VMEM] * 4,
+        [VMEM] * 3,
+        [pltpu.VMEM((half_rows, PIVOT), F32)],
+        waits=(s_own_far, own_sent),
+    )(tab_one, far_part, got_coup, inv_one, panel_own)
+    cross_a_far, cross_b_far = swap(cross_a, "hi"), swap(cross_b, "hi")
+    part = call(third_kernel, "second_front_part", tiles(G_NONE), [SMEM] + [VMEM] * 7, VMEM)(
+        tab_two, s_own, cross_a, cross_b, s_own_far, units, units_hi, rows_second
     )
-    quarter_rows = QUARTER * TILE
-    panel_two, schur_two = pl.pallas_call(
+    got_units = swap(after(units_sent, got_own, part), "lo")
+    s_oth, s_oth_sent = call(
+        add_kernel,
+        "first_front_last",
+        [tiles(N_TRI), dense(N_OWN * TILE + ROWS, TILE)],
+        [VMEM] * 2,
+        [VMEM] * 2,
+        waits=(part,),
+    )(s_part, got_own)
+    s_oth_far = swap(s_oth_sent, "hi")
+    units_both = swap(got_units, "hi")
+    got_two_a = swap(after(two_a, got_units, s_oth, cross_a_far, cross_b_far), "lo")
+    part = call(
+        more_kernel,
+        "second_front_more",
+        tiles(G_NONE),
+        [SMEM, HBM] + [VMEM] * 4,
+        VMEM,
+        [pltpu.SemaphoreType.DMA],
+    )(tab_two, part, cross_a_far, cross_b_far, s_oth, got_units)
+    got_two_b = swap(after(two_b, got_two_a, units_both, s_oth_far, part), "lo")
+    square = dense(SECOND, SECOND)
+    a, low, inv_a = call(
+        pivot_kernel,
+        "second_front_pivot",
+        [square] * 3,
+        [SMEM, HBM] + [VMEM] * 2,
+        [VMEM] * 3,
+        [
+            pltpu.VMEM((G_COUP, TILE, TILE), F32),
+            pltpu.VMEM((N_TRI, TILE, TILE), F32),
+            pltpu.SemaphoreType.DMA,
+        ],
+    )(tab_two, part, s_oth_far, units_both)
+    two_a_both = swap(got_two_a, "hi")
+    lower_two, inv_two = call(
+        pivot_rest_kernel,
+        "second_front_pivot_rest",
+        [dense(SECOND // 4, SECOND), square],
+        [SMEM] + [VMEM] * 3,
+        [VMEM] * 2,
+        [pltpu.VMEM((SECOND, SECOND), F32)] * 2,
+        waits=(got_two_a,),
+    )(tab_two, a, low, inv_a)
+    got_two_b = after(got_two_b, inv_two)
+    two_b_both = swap(got_two_b, "hi")
+    panel_two, schur, rest = call(
+        rows_kernel,
+        "second_front_rows",
+        [dense(WIDE, SECOND), dense(WIDE, U2T * TILE), dense(WIDE, SECOND)],
+        [SMEM, HBM] + [VMEM] * 6,
+        [VMEM] * 3,
+        [
+            pltpu.VMEM((G_NONE - G_COUP, TILE, TILE), F32),
+            pltpu.VMEM((N_TRI, TILE, TILE), F32),
+            pltpu.VMEM((3, WIDE, SECOND), F32),
+            pltpu.SemaphoreType.DMA,
+        ],
+    )(tab_two, part, s_oth_far, inv_two, two, got_two_a, got_two_b, two_hi)
+    schur_two = call(
         last_kernel,
-        out_shape=[dense(quarter_rows, SECOND), dense(quarter_rows, U2T * TILE)],
-        in_specs=[SMEM] + [VMEM] * 6,
-        out_specs=[VMEM] * 2,
-        scratch_shapes=[pltpu.VMEM((4, quarter_rows, SECOND), F32)],
-        name="second_front_rows",
-        compiler_params=params,
-        cost_estimate=cost(1000 * mega, 300),
-    )(tab_two, gathered, inv_two, coup_two, got_two, two_hi, two_both)
+        "second_front_last",
+        dense(WIDE, U2T * TILE),
+        [SMEM, HBM] + [VMEM] * 5,
+        HBM,
+        [pltpu.VMEM((WIDE, WIDE), F32), pltpu.SemaphoreType.DMA],
+        input_output_aliases={1: 0},
+    )(tab_two, schur, rest, panel_two, inv_two, two_a_both, two_b_both)
     return (
         lower_one[None, None],
         panel_one[None, None],

time: 782 us -> 406 us (0.52)
  Pallas kernels: 551 us -> 189 us
  other arithmetic: 21.9 us -> 5.45 us
    pallas_call x6 -> x17, Pallas kernels: 551 us -> 189 us  [the longest x11 189 us: call(): return lambda *args: run(*args, *waits)]
    select_n x4 -> x6, other arithmetic: 15 us -> 0.34 us  [the longest x2 0.16 us: slots(): jnp.where(row < P1T, pivot, jnp.where(col < P1T, coup, rest)).reshape(-1)]
    ppermute x12 -> x15, waiting for transfers between devices: 176 us -> 175 us  [swap(): return lax.ppermute(array, axis, [(i, i ^ size // 2) for i in range(size)])]
  transfers between devices with their start and end apart: 12 -> 15, of which waited for: 6 -> 8; matrix products, arithmetic and copies ran while one was open for 4% -> 3% of each run, Pallas kernels for 58% -> 44%
where the time goes in v2:
time: 406 us; the launch traced here: 401 us
  Pallas kernels  189 us (47%)
  waiting for transfers between devices  175 us (43%)
  local copies, waits for them, and re-layouts  16.1 us (4%)
  starting transfers between devices  14 us (3%)
  other arithmetic  5.45 us (1%)
    pallas_call x11, Pallas kernels, call(): return lambda *args: run(*args, *waits)  189 us
    ppermute x15, waiting for transfers between devices, swap(): return lax.ppermute(array, axis, [(i, i ^ size // 2) for i in range(size)])  175 us
    ppermute x15, starting transfers between devices, swap(): return lax.ppermute(array, axis, [(i, i ^ size // 2) for i in range(size)])  14 us
  transfers between devices with their start and end apart: 15, of which 8 were waited for; matrix products, arithmetic and copies ran while one was open for 3% of the time, Pallas kernels for 44%

profile of v2, /device:TPU:0, one launch (start us, length us, event | category | flops | bytes accessed | tf_op | source)
XLA Modules:
  0.0 401.4 jit_solution(5902966478755419918)
XLA Ops:
  0.7 0.7 fusion.15
  1.6 0.8 broadcast_add_fusion.15
  2.6 0.8 compare_select_fusion.2
  3.7 0.6 pad_add_fusion.refs_0_
  4.3 4.4 %pack_first.1.refs_6_ = f32[4744,128]{1,0:T(8,128)} custom-call(s32[9]{0:T(128)} %pad_add_fusion.refs_0_, f32[1024,1024]{1,0:T(8,128)} %bitcast.39, f32[384,768]{1,0:T(8,128)} %bitcast.44), custom_call_target="tpu_custom_call" | custom-call | flops 1 | bytes 1 | tf_op jit(solution)/shard_map/pack_first/pallas_call | solution.py:734
  8.7 4.1 %collective-permute-start = (f32[4744,128]{1,0:T(8,128)}, f32[4744,128]{1,0:T(8,128)S(1)}, u32[]{:S(2)}, u32[]{:S(2)}) collective-permute-start(f32[4744,128]{1,0:T(8,128)} %pack_first.1.refs_6_), channel_id=1, source_target_pairs={{0,16},{4,20},{8,24},{12,28},{16,0},{20,4},{24,8},{28,12},{1,17},{... | collective-permute-start | bytes 7286792 | tf_op jit(solution)/shard_map/ppermute | solution.py:699
  13.2 0.6 concatenate.14.refs_0_
  13.8 12.3 %pack_rest.1 = (f32[36,128,128]{2,1,0:T(8,128)}, f32[21,128,128]{2,1,0:T(8,128)}, f32[36,128,128]{2,1,0:T(8,128)}, f32[36,128,128]{2,1,0:T(8,128)}, f32[15,128,1...) custom-call(s32[30]{0:T(128)} %concatenate.14.refs_0_, ...), custom_call_target="tpu_custom_call" | custom-call | flops 1 | bytes 1 | tf_op jit(solution)/shard_map/pack_rest/pallas_call | solution.py:734
  26.1 1.5 collective-permute-start.1
  27.6 0.6 collective-permute-start.2
  31.1 0.6 dynamic_slice.29
  31.7 0.7 constant_dynamic-slice_fusion.1
  33.3 0.3 multiply_reduce_fusion
  33.7 1.3 dynamic_slice.24
  34.9 1.3 concatenate.13.refs_4_.refs_0_
  36.3 1.3 concatenate.16.refs_5_.refs_0_
  37.6 23.9 %collective-permute-done.2.refs_3_.refs_6_ = f32[704,128]{1,0:T(8,128)S(1)} collective-permute-done((f32[704,128]{1,0:T(8,128)}, f32[704,128]{1,0:T(8,128)S(1)}, u32[]{:S(2)}, u32[]{:S(2)}) %collective-permute-start.2) | collective-permute-done | bytes 360480 | tf_op jit(solution)/shard_map/ppermute | solution.py:699
  61.5 56.3 %collective-permute-done.refs_1_.refs_2_ = f32[4744,128]{1,0:T(8,128)S(1)} collective-permute-done((f32[4744,128]{1,0:T(8,128)}, f32[4744,128]{1,0:T(8,128)S(1)}, u32[]{:S(2)}, u32[]{:S(2)}) %collective-permute-start) | collective-permute-done | bytes 2428960 | tf_op jit(solution)/shard_map/ppermute | solution.py:699
  117.8 1.5 copy-done.1
  119.3 57.9 %first_front_own.1 = (f32[384,768]{1,0:T(8,128)}, f32[768,768]{1,0:T(8,128)}, f32[768,768]{1,0:T(8,128)}, f32[768,768]{1,0:T(8,128)}, f32[21,128,128]{2,1,0:T(8,128)}, /*index=5*/f32[93,128,128]{2,1,0:T(8,128)}) custom-call(s32[214]{0:T(256)} %concatenate.13.refs_4_.refs_0_, f32[36,128,128]{2,1,0:T(8,128)} %get-tuple-element.35.refs_1_, ...), custom_call_target="tpu_custom_call" | custom-call | flops 1 | bytes 1 | tf_op jit(solution)/shard_map/first_front_own/pallas_call | solution.py:734
  177.1 1.6 collective-permute-start.4
  178.8 44.6 %collective-permute-done.3.refs_1_.refs_2_ = f32[36,128,128]{2,1,0:T(8,128)S(1)} collective-permute-done((f32[36,128,128]{2,1,0:T(8,128)}, f32[36,128,128]{2,1,0:T(8,128)S(1)}, u32[]{:S(2)}, u32[]{:S(2)}) %collective-permute-start.3) | collective-permute-done | bytes 2359328 | tf_op jit(solution)/shard_map/ppermute | solution.py:699
  223.4 1.4 copy-done.2
  224.8 15.0 %first_front_other.1 = (f32[18,128,128]{2,1,0:T(8,128)}, f32[18,128,128]{2,1,0:T(8,128)}, f32[21,128,128]{2,1,0:T(8,128)}) custom-call(s32[214]{0:T(256)} %concatenate.13.refs_4_.refs_0_, f32[93,128,128]{2,1,0:T(8,128)} %get-tuple-element.45.refs_1_, f32[36,128,128]{2,1,0:T(8,128)} %copy-done.2, f32[768,768]{1,0:T(8,128)} %get-tuple-element.46.refs_3_, ...), custom_call_target="tpu_custom_call" | custom-call | flops 1 | bytes 1 | tf_op jit(solution)/shard_map/first_front_other/pallas_call | solution.py:734
  239.8 1.2 collective-permute-start.5
  241.0 0.8 collective-permute-start.6
  241.8 15.6 %second_front_part.1.refs_2_.refs_1_ = f32[144,128,128]{2,1,0:T(8,128)} custom-call(s32[653]{0:T(1024)} %concatenate.16.refs_5_.refs_0_, f32[21,128,128]{2,1,0:T(8,128)} %get-tuple-element.44.refs_1_, f32[18,128,128]{2,1,0:T(8,128)} %get-tuple-element.49.refs_2_, f32[18,128,128]{2,1,0:T(8,128)} %get-tuple-element.50.refs_3_, ...), custom_call_target="tpu_custom_call" | custom-call | flops 1 | bytes 1 | tf_op jit(solution)/shard_map/second_front_part/pallas_call | solution.py:734
  257.4 20.2 %collective-permute-done.7.refs_1_ = f32[2312,128]{1,0:T(8,128)S(1)} collective-permute-done((f32[2312,128]{1,0:T(8,128)}, f32[2312,128]{1,0:T(8,128)S(1)}, u32[]{:S(2)}, u32[]{:S(2)}) %collective-permute-start.7) | collective-permute-done | bytes 1183776 | tf_op jit(solution)/shard_map/ppermute | solution.py:699
  277.6 1.0 copy-done.4
  278.6 3.5 first_front_last.1
  282.1 0.9 collective-permute-start.9
  283.1 11.2 %collective-permute-done.6.refs_3_.refs_4_ = f32[18,128,128]{2,1,0:T(8,128)} collective-permute-done((f32[18,128,128]{2,1,0:T(8,128)}, f32[18,128,128]{2,1,0:T(8,128)}, u32[]{:S(2)}, u32[]{:S(2)}) %collective-permute-start.6) | collective-permute-done | bytes 1179680 | tf_op jit(solution)/shard_map/ppermute | solution.py:699
  294.3 6.2 %collective-permute-done.8.refs_5_.refs_1_ = f32[704,128]{1,0:T(8,128)S(1)} collective-permute-done((f32[704,128]{1,0:T(8,128)}, f32[704,128]{1,0:T(8,128)S(1)}, u32[]{:S(2)}, u32[]{:S(2)}) %collective-permute-start.8) | collective-permute-done | bytes 360480 | tf_op jit(solution)/shard_map/ppermute | solution.py:699
  300.5 0.8 copy-done.8
  301.2 1.1 collective-permute-start.10
  302.3 14.5 %second_front_more.1.refs_1_.refs_4_ = f32[144,128,128]{2,1,0:T(8,128)} custom-call(s32[653]{0:T(1024)} %concatenate.16.refs_5_.refs_0_, f32[144,128,128]{2,1,0:T(8,128)} %second_front_part.1.refs_2_.refs_1_, f32[18,128,128]{2,1,0:T(8,128)} %copy-done.5, f32[18,128,128]{2,1,0:T(8,128)} %collective-permute-done.6.refs_3_.refs_4_, ...), custom_call_target="tpu_custom_call" | custom-call | flops 1 | bytes 1 | tf_op jit(solution)/shard_map/second_front_more/pallas_call | solution.py:734
  316.9 7.7 %collective-permute-done.10.refs_3_.refs_2_ = f32[704,128]{1,0:T(8,128)S(1)} collective-permute-done((f32[704,128]{1,0:T(8,128)}, f32[704,128]{1,0:T(8,128)S(1)}, u32[]{:S(2)}, u32[]{:S(2)}) %collective-permute-start.10) | collective-permute-done | bytes 360480 | tf_op jit(solution)/shard_map/ppermute | solution.py:699
  324.6 5.1 %collective-permute-done.11.refs_4_.refs_1_.refs_5_ = f32[9,128,128]{2,1,0:T(8,128)S(1)} collective-permute-done((f32[9,128,128]{2,1,0:T(8,128)}, f32[9,128,128]{2,1,0:T(8,128)S(1)}, u32[]{:S(2)}, u32[]{:S(2)}) %collective-permute-start.11) | collective-permute-done | bytes 589856 | tf_op jit(solution)/shard_map/ppermute | solution.py:699
  329.7 0.8 copy-done.3
  330.5 0.4 copy-done
  330.9 1.4 collective-permute-start.13
  332.4 23.7 %second_front_pivot.1 = (f32[768,768]{1,0:T(8,128)}, f32[768,768]{1,0:T(8,128)}, f32[768,768]{1,0:T(8,128)}) custom-call(s32[653]{0:T(1024)} %concatenate.16.refs_5_.refs_0_, f32[144,128,128]{2,1,0:T(8,128)} %second_front_more.1.refs_1_.refs_4_, f32[2312,128]{1,0:T(8,128)} %copy-done, f32[704,128]{1,0:T(8,128)} %copy-done.7), custom_call_target="tpu_custom_call" | custom-call | flops 1 | bytes 1 | tf_op jit(solution)/shard_map/second_front_pivot/pallas_call | solution.py:734
  356.1 20.5 %second_front_pivot_rest.1 = (f32[192,768]{1,0:T(8,128)}, f32[768,768]{1,0:T(8,128)}) custom-call(s32[653]{0:T(1024)} %concatenate.16.refs_5_.refs_0_, f32[768,768]{1,0:T(8,128)} %get-tuple-element.55.refs_1_, f32[768,768]{1,0:T(8,128)} %get-tuple-element.56.refs_2_, f32[768,768]{1,0:T(8,128)} %get-tuple-element.57.refs_3_, f32[9,128,128]{2,1,0:T(8,128)} %copy-done.3), custom_call_target="tpu_custom_call" | custom-call | flops 1 | bytes 1 | tf_op jit(solution)/shard_map/second_front_pivot_rest/pallas_call | solution.py:734
  376.6 0.8 copy-done.6
  377.4 0.7 collective-permute-start.14
  378.1 14.8 %second_front_rows.1 = (f32[384,768]{1,0:T(8,128)}, f32[384,1536]{1,0:T(8,128)}, f32[384,768]{1,0:T(8,128)}) custom-call(s32[653]{0:T(1024)} %concatenate.16.refs_5_.refs_0_, f32[144,128,128]{2,1,0:T(8,128)} %second_front_more.1.refs_1_.refs_4_, f32[2312,128]{1,0:T(8,128)} %copy-done, f32[768,768]{1,0:T(8,128)} %get-tuple-element.60.refs_1_.refs_3_.refs_4_, ...), custom_call_target="tpu_custom_call" | custom-call | flops 1 | bytes 1 | tf_op jit(solution)/shard_map/second_front_rows/pallas_call | solution.py:734
  393.0 0.8 copy-done.10
  394.0 7.2 %second_front_last.1 = f32[384,1536]{1,0:T(8,128)} custom-call(s32[653]{0:T(1024)} %concatenate.16.refs_5_.refs_0_, f32[384,1536]{1,0:T(8,128)} %get-tuple-element.63.refs_1_, f32[384,768]{1,0:T(8,128)} %get-tuple-element.64.refs_2_, f32[384,768]{1,0:T(8,128)} %get-tuple-element.62.refs_3_, ...), custom_call_target="tpu_custom_call", output_to_operand_aliasing={{}: (1, {})} | custom-call | flops 1 | bytes 1 | tf_op jit(solution)/shard_map/second_front_last/pallas_call | solution.py:734
  (93 shorter events, 5.0 us)
Async XLA Ops:
  8.7 109.1 %collective-permute-start = (f32[4744,128]{1,0:T(8,128)}, f32[4744,128]{1,0:T(8,128)S(1)}, u32[]{:S(2)}, u32[]{:S(2)}) collective-permute-start(f32[4744,128]{1,0:T(8,128)} %pack_first.1.refs_6_), channel_id=1, source_target_pairs={{0,16},{4,20},{8,24},{12,28},{16,0},{20,4},{24,8},{28,12},{1,17},{... | collective-permute-start | bytes 7286792 | tf_op jit(solution)/shard_map/ppermute | solution.py:699
  13.8 17.2 %copy-start.12 = (s32[2,4]{1,0:T(2,128)S(1)}, s32[2,4]{1,0:T(2,128)}, u32[]{:S(2)}) copy-start(s32[2,4]{1,0:T(2,128)} %param.21) | copy-start | bytes 100
  26.1 35.4 %collective-permute-start.1 = (f32[18,128,128]{2,1,0:T(8,128)}, f32[18,128,128]{2,1,0:T(8,128)}, u32[]{:S(2)}, u32[]{:S(2)}) collective-permute-start(f32[18,128,128]{2,1,0:T(8,128)} %get-tuple-element.37.refs_4_), channel_id=1, source_target_pairs={{0,2},{1,3},{2,0},{3,1},{4,6},{5,7},{6,4},{7,5},{8,10},{9,11},{10,... | collective-permute-start | bytes 3538952 | tf_op jit(solution)/shard_map/ppermute | solution.py:699
  27.6 33.9 %collective-permute-start.2 = (f32[704,128]{1,0:T(8,128)}, f32[704,128]{1,0:T(8,128)S(1)}, u32[]{:S(2)}, u32[]{:S(2)}) collective-permute-start(f32[704,128]{1,0:T(8,128)} %get-tuple-element.38.refs_5_), channel_id=1, source_target_pairs={{0,2},{1,3},{2,0},{3,1},{4,6},{5,7},{6,4},{7,5},{8,10},{9,11},{10,... | collective-permute-start | bytes 1081352 | tf_op jit(solution)/shard_map/ppermute | solution.py:699
  61.5 56.3 %copy-start.9 = (f32[704,128]{1,0:T(8,128)}, f32[704,128]{1,0:T(8,128)S(1)}, u32[]{:S(2)}) copy-start(f32[704,128]{1,0:T(8,128)S(1)} %collective-permute-done.2.refs_3_.refs_6_) | copy-start | bytes 1081348
  117.8 1.5 copy-start.1
  119.3 104.1 %collective-permute-start.3 = (f32[36,128,128]{2,1,0:T(8,128)}, f32[36,128,128]{2,1,0:T(8,128)S(1)}, u32[]{:S(2)}, u32[]{:S(2)}) collective-permute-start(f32[36,128,128]{2,1,0:T(8,128)} %after.6.refs_3_), channel_id=1, source_target_pairs={{0,16},{4,20},{8,24},{12,28},{16,0},{20,4},{24,8},{28,12},{1,17},{... | collective-permute-start | bytes 7077896 | tf_op jit(solution)/shard_map/ppermute | solution.py:699
  177.1 47.6 %collective-permute-start.4 = (f32[21,128,128]{2,1,0:T(8,128)}, f32[21,128,128]{2,1,0:T(8,128)}, u32[]{:S(2)}, u32[]{:S(2)}) collective-permute-start(f32[21,128,128]{2,1,0:T(8,128)} %get-tuple-element.44.refs_1_), channel_id=1, source_target_pairs={{0,2},{1,3},{2,0},{3,1},{4,6},{5,7},{6,4},{7,5},{8,10},{9,11},{10,... | collective-permute-start | bytes 4128776 | tf_op jit(solution)/shard_map/ppermute | solution.py:699
  223.4 1.4 copy-start.2
  224.8 52.8 %collective-permute-start.7 = (f32[2312,128]{1,0:T(8,128)}, f32[2312,128]{1,0:T(8,128)S(1)}, u32[]{:S(2)}, u32[]{:S(2)}) collective-permute-start(f32[2312,128]{1,0:T(8,128)} %after.7.refs_6_), channel_id=1, source_target_pairs={{0,16},{4,20},{8,24},{12,28},{16,0},{20,4},{24,8},{28,12},{1,17},{... | collective-permute-start | bytes 3551240 | tf_op jit(solution)/shard_map/ppermute | solution.py:699
  239.8 43.3 %collective-permute-start.5 = (f32[18,128,128]{2,1,0:T(8,128)}, f32[18,128,128]{2,1,0:T(8,128)S(1)}, u32[]{:S(2)}, u32[]{:S(2)}) collective-permute-start(f32[18,128,128]{2,1,0:T(8,128)} %get-tuple-element.49.refs_2_), channel_id=1, source_target_pairs={{0,2},{1,3},{2,0},{3,1},{4,6},{5,7},{6,4},{7,5},{8,10},{9,11},{10,... | collective-permute-start | bytes 3538952 | tf_op jit(solution)/shard_map/ppermute | solution.py:699
  241.0 53.3 %collective-permute-start.6 = (f32[18,128,128]{2,1,0:T(8,128)}, f32[18,128,128]{2,1,0:T(8,128)}, u32[]{:S(2)}, u32[]{:S(2)}) collective-permute-start(f32[18,128,128]{2,1,0:T(8,128)} %get-tuple-element.50.refs_3_), channel_id=1, source_target_pairs={{0,2},{1,3},{2,0},{3,1},{4,6},{5,7},{6,4},{7,5},{8,10},{9,11},{10,... | collective-permute-start | bytes 3538952 | tf_op jit(solution)/shard_map/ppermute | solution.py:699
  277.6 1.0 copy-start.4
  282.1 47.6 %collective-permute-start.9 = (f32[2312,128]{1,0:T(8,128)}, f32[2312,128]{1,0:T(8,128)S(1)}, u32[]{:S(2)}, u32[]{:S(2)}) collective-permute-start(f32[2312,128]{1,0:T(8,128)} %get-tuple-element.54), channel_id=1, source_target_pairs={{0,2},{1,3},{2,0},{3,1},{4,6},{5,7},{6,4},{7,5},{8,10},{9,11},{10,... | collective-permute-start | bytes 3551240 | tf_op jit(solution)/shard_map/ppermute | solution.py:699
  283.1 17.4 %collective-permute-start.8 = (f32[704,128]{1,0:T(8,128)}, f32[704,128]{1,0:T(8,128)S(1)}, u32[]{:S(2)}, u32[]{:S(2)}) collective-permute-start(f32[704,128]{1,0:T(8,128)} %after.8), channel_id=1, source_target_pairs={{0,16},{4,20},{8,24},{12,28},{16,0},{20,4},{24,8},{28,12},{1,17},{... | collective-permute-start | bytes 1081352 | tf_op jit(solution)/shard_map/ppermute | solution.py:699
  283.1 17.4 %copy-start.5 = (f32[18,128,128]{2,1,0:T(8,128)}, f32[18,128,128]{2,1,0:T(8,128)S(1)}, u32[]{:S(2)}) copy-start(f32[18,128,128]{2,1,0:T(8,128)S(1)} %collective-permute-done.5.refs_2_.refs_3_) | copy-start | bytes 3538948
  300.5 0.8 copy-start.8
  301.2 28.4 %collective-permute-start.11 = (f32[9,128,128]{2,1,0:T(8,128)}, f32[9,128,128]{2,1,0:T(8,128)S(1)}, u32[]{:S(2)}, u32[]{:S(2)}) collective-permute-start(f32[9,128,128]{2,1,0:T(8,128)} %after.9), channel_id=1, source_target_pairs={{0,16},{4,20},{8,24},{12,28},{16,0},{20,4},{24,8},{28,12},{1,17},{... | collective-permute-start | bytes 1769480 | tf_op jit(solution)/shard_map/ppermute | solution.py:699
  301.2 23.3 %collective-permute-start.10 = (f32[704,128]{1,0:T(8,128)}, f32[704,128]{1,0:T(8,128)S(1)}, u32[]{:S(2)}, u32[]{:S(2)}) collective-permute-start(f32[704,128]{1,0:T(8,128)} %copy-done.8), channel_id=1, source_target_pairs={{0,2},{1,3},{2,0},{3,1},{4,6},{5,7},{6,4},{7,5},{8,10},{9,11},{10,... | collective-permute-start | bytes 1081352 | tf_op jit(solution)/shard_map/ppermute | solution.py:699
  324.6 5.1 %copy-start.7 = (f32[704,128]{1,0:T(8,128)}, f32[704,128]{1,0:T(8,128)S(1)}, u32[]{:S(2)}) copy-start(f32[704,128]{1,0:T(8,128)S(1)} %collective-permute-done.10.refs_3_.refs_2_) | copy-start | bytes 1081348
  329.7 0.9 copy-start.3
  329.7 1.2 copy-start
  330.9 45.6 %collective-permute-start.12 = (f32[9,128,128]{2,1,0:T(8,128)}, f32[9,128,128]{2,1,0:T(8,128)S(1)}, u32[]{:S(2)}, u32[]{:S(2)}) collective-permute-start(f32[9,128,128]{2,1,0:T(8,128)} %after.10), channel_id=1, source_target_pairs={{0,16},{4,20},{8,24},{12,28},{16,0},{20,4},{24,8},{28,12},{1,17},{... | collective-permute-start | bytes 1769480 | tf_op jit(solution)/shard_map/ppermute | solution.py:699
  330.9 62.0 %collective-permute-start.13 = (f32[9,128,128]{2,1,0:T(8,128)}, f32[9,128,128]{2,1,0:T(8,128)S(1)}, u32[]{:S(2)}, u32[]{:S(2)}) collective-permute-start(f32[9,128,128]{2,1,0:T(8,128)} %copy-done.3), channel_id=1, source_target_pairs={{0,2},{1,3},{2,0},{3,1},{4,6},{5,7},{6,4},{7,5},{8,10},{9,11},{10,... | collective-permute-start | bytes 1769480 | tf_op jit(solution)/shard_map/ppermute | solution.py:699
  376.6 0.8 copy-start.6
  377.4 15.5 %collective-permute-start.14 = (f32[9,128,128]{2,1,0:T(8,128)}, f32[9,128,128]{2,1,0:T(8,128)S(1)}, u32[]{:S(2)}, u32[]{:S(2)}) collective-permute-start(f32[9,128,128]{2,1,0:T(8,128)} %after.11.refs_6_), channel_id=1, source_target_pairs={{0,2},{1,3},{2,0},{3,1},{4,6},{5,7},{6,4},{7,5},{8,10},{9,11},{10,... | collective-permute-start | bytes 1769480 | tf_op jit(solution)/shard_map/ppermute | solution.py:699
  392.9 0.8 copy-start.10
  392.9 1.0 copy-start.11
